TPU v7x, 512 devices: a whole 4x8x8 slice. The times are simulated.
512 devices in a mesh: seq: 32 (over y_lo, z), head: 16 (over y_hi, x, core).
Axes of the slice: x: 4, y: 8 (y_hi: 2, y_lo: 4; y = y_hi * 4 + y_lo), z: 8, core: 2. Of those that a mesh axis runs over, the one named last changes fastest.
Arguments:
- queries: bfloat16 [65536, 4096], P(('seq', 'head')), may hold values from -6 to 6
- out_grad: bfloat16 [65536, 4096], P(('seq', 'head')), may hold values from -24 to 24
- latents: bfloat16 [32, 64, 1280], P('seq'), may hold values from -6 to 6
- key_weight: bfloat16 [1280, 4096], P(None, 'head'), may hold values from -0.15625 to 0.15625
- value_weight: bfloat16 [1280, 4096], P(None, 'head'), may hold values from -0.15625 to 0.15625
- query_gain: float32 [128], replicated, may hold values from 0.25 to 1.75
- key_gain: float32 [128], replicated, may hold values from 0.25 to 1.75
- gate_alpha: float32 [1], replicated, may hold values from 0.5 to 1.5
- media_slot: int32 [32], replicated, may hold values from 0 to 31, each once
- media_position: int32 [32], replicated, may hold values from 0 to 65535, as said below
- tile_list: int32 [128, 8], P('seq'), may hold values from -1 to 31, as said below
Outputs:
- grad_queries: bfloat16 [65536, 4096], P(('seq', 'head'))
- grad_latents: bfloat16 [32, 64, 1280], P('seq', 'head')
- grad_key_weight: float32 [1280, 4096], P('seq', 'head')
- grad_value_weight: float32 [1280, 4096], P('seq', 'head')
Inputs may be any that keep to these rules, and one draw needn't show every extreme that they name: `tile_list`: row i names, in increasing order, consecutive image numbers: the images of tile i's document with media_position below (i + 1) * 512 - 1, then -1 in the remaining entries. Documents cover whole tiles. Every image is named by some row. `media_position`: strictly increasing in the image number; an image lies within the tokens of its document.
All inputs are finite; a program needn't handle non-finite values.
Results may differ from a plain program's by a relative error of at most 0.035.
Values may be sent and summed in bfloat16 or wider, within the bound.
A program may use at most 64 MiB of HBM per device.

v0:
```python
import jax
import jax.numpy as jnp
from jax import lax
from jax.sharding import PartitionSpec as P

HD = 128


EPS = 1e-06


def head_norm(raw_rows, gain_row):
    inverse = lax.rsqrt(jnp.mean(raw_rows * raw_rows, axis=-1, keepdims=True) + EPS)
    return (raw_rows * inverse * gain_row, inverse)


def norm_back(upstream, raw_rows, inverse, gain_row):
    scaled = upstream * gain_row
    row_inner = jnp.mean(scaled * raw_rows, axis=-1, keepdims=True)
    return inverse * (scaled - raw_rows * inverse * inverse * row_inner)


def project(image_rows, key_weight, value_weight, key_gain):
    block_rows = image_rows.shape[0]
    latent = image_rows.shape[1]
    local_width = key_weight.shape[1]
    flat_rows = image_rows.reshape(block_rows * latent, image_rows.shape[2])
    raw_rows = jnp.dot(flat_rows, key_weight, preferred_element_type=jnp.float32).reshape(
        block_rows * latent, local_width // HD, HD
    )
    normed, inverse = head_norm(raw_rows, key_gain)
    keys_out = normed.astype(jnp.bfloat16).reshape(block_rows, latent, local_width)
    values_out = (
        jnp.dot(flat_rows, value_weight, preferred_element_type=jnp.float32)
        .astype(jnp.bfloat16)
        .reshape(block_rows, latent, local_width)
    )
    return (keys_out, values_out, raw_rows, inverse)


def place(buffers, pieces, slot_ids):
    block_rows = pieces[0].shape[0]
    select = (slot_ids[:, None] == jnp.arange(block_rows, dtype=jnp.int32)[None, :]).astype(
        jnp.bfloat16
    )
    filled = []
    for buffer, piece_rows in zip(buffers, pieces):
        placed = jnp.dot(
            select, piece_rows.reshape(block_rows, -1), preferred_element_type=jnp.float32
        )
        filled.append(placed.astype(jnp.bfloat16))
    return tuple(filled)


def body(
    queries,
    out_grad,
    latents,
    key_weight,
    value_weight,
    query_gain,
    key_gain,
    gate_alpha,
    media_slot,
    media_position,
    tile_list,
):
    head_count = lax.axis_size("head")
    seq_place = lax.axis_index("seq")
    local_width = key_weight.shape[1]
    local_heads = local_width // HD
    token_rows = queries.shape[0] * head_count
    tile_count = tile_list.shape[0]
    tile_rows = token_rows // tile_count
    list_width = tile_list.shape[1]
    image_count = media_slot.shape[0]
    own_images = latents.shape[0]
    latent_rows = latents.shape[1]
    vision_width = latents.shape[2]
    entry_count = tile_count * list_width
    scale_factor = HD ** (-0.5)
    gate_value = jnp.tanh(gate_alpha[0])
    entry_ids = tile_list.reshape(entry_count)
    entry_live = entry_ids >= 0
    image_range = jnp.arange(image_count, dtype=jnp.int32)
    matches = entry_ids[:, None] == image_range[None, :]
    entry_slot = jnp.where(
        entry_live, jnp.sum(jnp.where(matches, media_slot[None, :], 0), axis=1), -1
    )
    entry_place = jnp.sum(jnp.where(matches, media_position[None, :], 0), axis=1)
    own_keys, own_values, own_raw, own_inverse = project(
        latents, key_weight, value_weight, key_gain
    )
    empty_buffer = jnp.zeros((entry_count, latent_rows * local_width), jnp.bfloat16)
    query_rows, grad_rows = (
        lax.all_to_all(queries, "head", split_axis=1, concat_axis=0, tiled=True),
        lax.all_to_all(out_grad, "head", split_axis=1, concat_axis=0, tiled=True),
    )
    piece_keys, piece_values, unused_raw, unused_inverse = project(
        lax.all_gather(latents, "seq", axis=0, tiled=True), key_weight, value_weight, key_gain
    )
    key_buffer, value_buffer = place(
        (empty_buffer, empty_buffer), (piece_keys, piece_values), entry_slot
    )
    query_tiles = query_rows.reshape(tile_count, tile_rows, local_heads, HD)
    grad_tiles = grad_rows.reshape(tile_count, tile_rows, local_heads, HD)
    key_tiles = key_buffer.reshape(tile_count, list_width * latent_rows, local_heads, HD)
    value_tiles = value_buffer.reshape(tile_count, list_width * latent_rows, local_heads, HD)
    live_tiles = entry_live.reshape(tile_count, list_width)
    place_tiles = entry_place.reshape(tile_count, list_width)
    tile_ids = jnp.arange(tile_count, dtype=jnp.int32)

    def attend(inputs):
        query_tile, grad_tile, key_tile, value_tile, live_tile, place_tile, tile_index = inputs
        token_places = (
            seq_place * token_rows + tile_index * tile_rows + jnp.arange(tile_rows, dtype=jnp.int32)
        )
        entry_ok = live_tile[None, :] & (place_tile[None, :] < token_places[:, None])
        key_ok = jnp.repeat(entry_ok, latent_rows, axis=1)
        has_key = jnp.any(entry_ok, axis=1)
        query_full = query_tile.astype(jnp.float32)
        query_hat, query_inverse = head_norm(query_full, query_gain)
        query_hat = query_hat.astype(jnp.bfloat16)
        scores = (
            jnp.einsum("qhd,khd->hqk", query_hat, key_tile, preferred_element_type=jnp.float32)
            * scale_factor
        )
        exp_scores = jnp.where(key_ok[None], jnp.exp(scores), 0.0)
        denominator = (
            jnp.sum(exp_scores, axis=2, keepdims=True) + jnp.where(has_key, 0.0, 1.0)[None, :, None]
        )
        probs = (exp_scores / denominator).astype(jnp.bfloat16)
        grad_ctx = (gate_value * grad_tile.astype(jnp.float32)).astype(jnp.bfloat16)
        grad_probs = jnp.einsum(
            "qhd,khd->hqk", grad_ctx, value_tile, preferred_element_type=jnp.float32
        )
        probs_full = probs.astype(jnp.float32)
        row_inner = jnp.sum(probs_full * grad_probs, axis=2, keepdims=True)
        grad_scores = (probs_full * (grad_probs - row_inner) * scale_factor).astype(jnp.bfloat16)
        grad_qhat = jnp.einsum(
            "hqk,khd->qhd", grad_scores, key_tile, preferred_element_type=jnp.float32
        )
        grad_query = norm_back(grad_qhat, query_full, query_inverse, query_gain).astype(
            jnp.bfloat16
        )
        grad_key = jnp.einsum(
            "hqk,qhd->khd", grad_scores, query_hat, preferred_element_type=jnp.float32
        )
        grad_value = jnp.einsum("hqk,qhd->khd", probs, grad_ctx, preferred_element_type=jnp.float32)
        return (
            grad_query.reshape(tile_rows, local_width),
            grad_key.reshape(list_width, latent_rows * local_width),
            grad_value.reshape(list_width, latent_rows * local_width),
        )

    tile_inputs = (
        query_tiles,
        grad_tiles,
        key_tiles,
        value_tiles,
        live_tiles,
        place_tiles,
        tile_ids,
    )
    grad_queries, grad_keys, grad_values = lax.map(attend, tile_inputs)
    slot_hits = (image_range[:, None] == entry_slot[None, :]).astype(jnp.float32)
    key_part = jnp.dot(
        slot_hits,
        grad_keys.reshape(entry_count, latent_rows * local_width),
        precision=lax.Precision.HIGHEST,
    )
    value_part = jnp.dot(
        slot_hits,
        grad_values.reshape(entry_count, latent_rows * local_width),
        precision=lax.Precision.HIGHEST,
    )
    key_part = key_part.reshape(image_count, latent_rows, local_width)
    value_part = value_part.reshape(image_count, latent_rows, local_width)
    key_sum, value_sum = (
        lax.psum_scatter(
            key_part.astype(jnp.bfloat16), "seq", scatter_dimension=0, tiled=True
        ).astype(jnp.float32),
        lax.psum_scatter(
            value_part.astype(jnp.bfloat16), "seq", scatter_dimension=0, tiled=True
        ).astype(jnp.float32),
    )
    key_sum = key_sum.reshape(own_images * latent_rows, local_heads, HD)
    raw_grad = (
        norm_back(key_sum, own_raw, own_inverse, key_gain)
        .astype(jnp.bfloat16)
        .reshape(own_images * latent_rows, local_width)
    )
    value_grad = value_sum.reshape(own_images * latent_rows, local_width).astype(jnp.bfloat16)
    latent_term = jnp.einsum(
        "rf,cf->rc", raw_grad, key_weight, preferred_element_type=jnp.float32
    ) + jnp.einsum("rf,cf->rc", value_grad, value_weight, preferred_element_type=jnp.float32)
    latent_term = latent_term.reshape(own_images, latent_rows, vision_width)
    latent_grad = lax.psum_scatter(
        latent_term.astype(jnp.bfloat16), "head", scatter_dimension=1, tiled=True
    )
    both_grads = jnp.concatenate([raw_grad, value_grad], axis=1)
    latent_flat = latents.reshape(own_images * latent_rows, vision_width)
    weight_share = lax.psum_scatter(
        jnp.einsum("rc,rf->cf", latent_flat, both_grads, preferred_element_type=jnp.float32).astype(
            jnp.bfloat16
        ),
        "seq",
        scatter_dimension=0,
        tiled=True,
    ).astype(jnp.float32)
    key_weight_grad = weight_share[:, :local_width]
    value_weight_grad = weight_share[:, local_width:]
    query_grad = lax.all_to_all(
        grad_queries.reshape(token_rows, local_width),
        "head",
        split_axis=0,
        concat_axis=1,
        tiled=True,
    )
    return (query_grad, latent_grad, key_weight_grad, value_weight_grad)


def solution(mesh):
    in_specs = (
        P(("seq", "head"), None),
        P(("seq", "head"), None),
        P("seq", None, None),
        P(None, "head"),
        P(None, "head"),
        P(),
        P(),
        P(),
        P(),
        P(),
        P("seq", None),
    )
    out_specs = (
        P(("seq", "head"), None),
        P("seq", "head", None),
        P("seq", "head"),
        P("seq", "head"),
    )
    return jax.shard_map(body, mesh=mesh, in_specs=in_specs, out_specs=out_specs, check_vma=False)
```

profile of v0, /device:TPU:56, one launch (start us, length us, event | category | flops | bytes accessed | tf_op | source)
XLA Modules:
  0.0 964.6 jit_solution(9529426551314277123)
XLA Ops:
  10.3 9.7 %all-to-all-start = ((bf16[128,16,256]{2,0,1:T(8,128)(2,1)}), bf16[128,16,256]{2,0,1:T(8,128)(2,1)S(1)}, u32[]{:S(2)}, u32[]{:S(2)}) async-start(bf16[128,16,256]{2,0,1:T(8,128)(2,1)} %bitcast.115), calls=%async_computation | async-start | bytes 2097152 | tf_op jit(solution)/shard_map/all_to_all | solution.py:96
  21.1 16.8 %all-to-all-done = bf16[128,16,256]{2,0,1:T(8,128)(2,1)S(1)} async-done(((bf16[128,16,256]{2,0,1:T(8,128)(2,1)}), bf16[128,16,256]{2,0,1:T(8,128)(2,1)S(1)}, u32[]{:S(2)}, u32[]{:S(2)}) %all-to-all-start) | async-done | bytes 1048608 | tf_op jit(solution)/shard_map/all_to_all | solution.py:96
  37.9 9.9 %all-to-all-start.1 = ((bf16[128,16,256]{2,0,1:T(8,128)(2,1)}), bf16[128,16,256]{2,0,1:T(8,128)(2,1)S(1)}, u32[]{:S(2)}, u32[]{:S(2)}) async-start(bf16[128,16,256]{2,0,1:T(8,128)(2,1)} %bitcast.114), calls=%async_computation.1 | async-start | bytes 2097152 | tf_op jit(solution)/shard_map/all_to_all | solution.py:97
  51.7 28.3 %all-to-all-done.1 = bf16[128,16,256]{2,0,1:T(8,128)(2,1)S(1)} async-done(((bf16[128,16,256]{2,0,1:T(8,128)(2,1)}), bf16[128,16,256]{2,0,1:T(8,128)(2,1)S(1)}, u32[]{:S(2)}, u32[]{:S(2)}) %all-to-all-start.1) | async-done | bytes 1048608 | tf_op jit(solution)/shard_map/all_to_all | solution.py:97
  80.3 102.4 %all-gather.2.cloned.1.call-done = bf16[32,64,1280]{2,1,0:T(8,128)(2,1)} async-done(((bf16[1,64,1280]{2,1,0:T(8,128)(2,1)}), bf16[32,64,1280]{2,1,0:T(8,128)(2,1)}) %all-gather.2.cloned.1.call-update) | async-done | bytes 5242896 | tf_op jit(solution)/shard_map/all_gather | solution.py:100
  182.7 4.1 multiply_reduce_fusion
  192.5 2.6 reshape.178
  195.1 5.0 convolution_convert_fusion.3
  206.2 82.4 %while.16 = (s32[]{:T(128)}, bf16[4,512,256]{2,1,0:T(8,128)(2,1)}, f32[4,8,16384]{2,1,0:T(8,128)}, f32[4,8,16384]{2,1,0:T(8,128)}, bf16[4,512,2,128]{3,2,1,0:T(2...) while((s32[]{:T(128)}, bf16[4,512,256]{2,1,0:T(8,128)(2,1)}, ...), condition=%wide.region_9.10_spmd, body=%wide.region_3.9_spmd.sunk | while | flops 685785600 | bytes 38874012 | solution.py:165
  216.8 3.1 fusion.104
  222.0 3.0 fusion.106
  237.3 3.1 fusion.104
  242.6 3.0 fusion.106
  257.9 3.1 fusion.104
  263.2 3.0 fusion.106
  278.6 3.1 fusion.104
  283.8 3.0 fusion.106
  288.7 2.7 fusion.43
  295.9 151.9 %reduce-scatter.7.cloned.1.call-done = bf16[1,64,256]{2,1,0:T(8,128)(2,1)} async-done(((bf16[32,64,256]{2,1,0:T(8,128)(2,1)}), bf16[1,64,256]{2,1,0:T(8,128)(2,1)}) %reduce-scatter.7.cloned.1.call-update) | async-done | bytes 32784 | tf_op jit(solution)/shard_map/reduce_scatter | solution.py:180
  449.6 157.0 %reduce-scatter.9.cloned.1.call-done = bf16[1,64,256]{2,1,0:T(8,128)(2,1)} async-done(((bf16[32,64,256]{2,1,0:T(8,128)(2,1)}), bf16[1,64,256]{2,1,0:T(8,128)(2,1)}) %reduce-scatter.9.cloned.1.call-update) | async-done | bytes 32784 | tf_op jit(solution)/shard_map/reduce_scatter | solution.py:183
  611.2 9.9 %all-to-all-start.2 = ((bf16[16,128,256]{2,1,0:T(8,128)(2,1)}), bf16[16,128,256]{2,1,0:T(8,128)(2,1)S(1)}, u32[]{:S(2)}, u32[]{:S(2)}) async-start(bf16[16,128,256]{2,1,0:T(8,128)(2,1)} %bitcast.19), calls=%async_computation.2 | async-start | bytes 2097152 | tf_op jit(solution)/shard_map/all_to_all | solution.py:213
  623.1 19.8 %all-to-all-done.2 = bf16[16,128,256]{2,1,0:T(8,128)(2,1)S(1)} async-done(((bf16[16,128,256]{2,1,0:T(8,128)(2,1)}), bf16[16,128,256]{2,1,0:T(8,128)(2,1)S(1)}, u32[]{:S(2)}, u32[]{:S(2)}) %all-to-all-start.2) | async-done | bytes 1048608 | tf_op jit(solution)/shard_map/all_to_all | solution.py:213
  644.9 159.5 %all-reduce.3.cloned.1.call-done = bf16[1,64,1280]{2,1,0:T(8,128)(2,1)} async-done(((bf16[1,64,1280]{2,1,0:T(8,128)(2,1)}), bf16[1,64,1280]{2,1,0:T(8,128)(2,1)}) %all-reduce.3.cloned.1.call-update) | async-done | bytes 163856
  805.7 150.0 %reduce-scatter.11.cloned.1.call-done = bf16[40,512]{1,0:T(8,128)(2,1)} async-done(((bf16[1280,512]{1,0:T(8,128)(2,1)}), bf16[40,512]{1,0:T(8,128)(2,1)}) %reduce-scatter.11.cloned.1.call-update) | async-done | bytes 40976
  (203 shorter events, 91.8 us)
Async XLA Ops:
  7.2 187.9 %copy-start = (bf16[1280,256]{1,0:T(8,128)(2,1)S(1)}, bf16[1280,256]{1,0:T(8,128)(2,1)}, u32[]{:S(2)}) copy-start(bf16[1280,256]{1,0:T(8,128)(2,1)} %param.17) | copy-start | bytes 1966084
  7.2 175.5 %all-gather.2.cloned.1.call-start = ((), (), s32[]{:S(2)}) async-start(), calls=%async_computation.6 | async-start | bytes 5406720 | tf_op jit(solution)/shard_map/all_gather | solution.py:100
  7.9 12.1 %copy-start.9 = (bf16[128,4096]{1,0:T(8,128)(2,1)S(1)}, bf16[128,4096]{1,0:T(8,128)(2,1)}, u32[]{:S(2)}) copy-start(bf16[128,4096]{1,0:T(8,128)(2,1)} %param.14) | copy-start | bytes 3145732
  10.3 27.6 %all-to-all-start = ((bf16[128,16,256]{2,0,1:T(8,128)(2,1)}), bf16[128,16,256]{2,0,1:T(8,128)(2,1)S(1)}, u32[]{:S(2)}, u32[]{:S(2)}) async-start(bf16[128,16,256]{2,0,1:T(8,128)(2,1)} %bitcast.115), calls=%async_computation | async-start | bytes 2097152 | tf_op jit(solution)/shard_map/all_to_all | solution.py:96
  20.0 27.9 %copy-start.3 = (bf16[1280,256]{1,0:T(8,128)(2,1)S(1)}, bf16[1280,256]{1,0:T(8,128)(2,1)}, u32[]{:S(2)}) copy-start(bf16[1280,256]{1,0:T(8,128)(2,1)} %param.16) | copy-start | bytes 1966084
  21.1 28.0 %copy-start.10 = (s32[4,8]{1,0:T(4,128)S(1)}, s32[4,8]{1,0:T(4,128)}, u32[]{:S(2)}) copy-start(s32[4,8]{1,0:T(4,128)} %param.23) | copy-start | bytes 388
  21.1 28.0 %copy-start.12 = (s32[32]{0:T(128)S(1)}, s32[32]{0:T(128)}, u32[]{:S(2)}) copy-start(s32[32]{0:T(128)} %param.22) | copy-start | bytes 388
  21.1 28.0 %copy-start.13 = (s32[32]{0:T(128)S(1)}, s32[32]{0:T(128)}, u32[]{:S(2)}) copy-start(s32[32]{0:T(128)} %param.21) | copy-start | bytes 388
  37.9 42.1 %all-to-all-start.1 = ((bf16[128,16,256]{2,0,1:T(8,128)(2,1)}), bf16[128,16,256]{2,0,1:T(8,128)(2,1)S(1)}, u32[]{:S(2)}, u32[]{:S(2)}) async-start(bf16[128,16,256]{2,0,1:T(8,128)(2,1)} %bitcast.114), calls=%async_computation.1 | async-start | bytes 2097152 | tf_op jit(solution)/shard_map/all_to_all | solution.py:97
  47.8 400.0 %reduce-scatter.7.cloned.1.call-start = ((), (), s32[]{:S(2)}) async-start(), calls=%async_computation.7 | async-start | bytes 1081344 | tf_op jit(solution)/shard_map/reduce_scatter | solution.py:180
  50.6 132.1 %copy-start.5 = (bf16[256,1280]{1,0:T(8,128)(2,1)S(1)}, bf16[256,1280]{1,0:T(8,128)(2,1)}, u32[]{:S(2)}) copy-start(bf16[256,1280]{1,0:T(8,128)(2,1)} %copy.143) | copy-start | bytes 1966084
  182.7 4.1 copy-start.11
  206.2 8.5 copy-start.1
  226.8 8.5 copy-start.1
  247.4 8.5 copy-start.1
  268.0 8.5 copy-start.1
  291.4 1.7 copy-start.7
  293.0 313.6 %reduce-scatter.9.cloned.1.call-start = ((), (), s32[]{:S(2)}) async-start(), calls=%async_computation.8 | async-start | bytes 1081344 | tf_op jit(solution)/shard_map/reduce_scatter | solution.py:183
  294.2 154.5 %copy-start.6 = (bf16[256,1280]{1,0:T(8,128)(2,1)S(1)}, bf16[256,1280]{1,0:T(8,128)(2,1)}, u32[]{:S(2)}) copy-start(bf16[256,1280]{1,0:T(8,128)(2,1)} %copy.143) | copy-start | bytes 1966084
  294.2 154.5 %copy-start.8 = (bf16[1,64,1280]{2,1,0:T(8,128)(2,1)S(1)}, bf16[1,64,1280]{2,1,0:T(8,128)(2,1)}, u32[]{:S(2)}) copy-start(bf16[1,64,1280]{2,1,0:T(8,128)(2,1)} %param.15) | copy-start | bytes 491524
  294.2 155.0 %copy-start.4 = (bf16[1280,256]{1,0:T(8,128)(2,1)S(1)}, bf16[1280,256]{1,0:T(8,128)(2,1)}, u32[]{:S(2)}) copy-start(bf16[1280,256]{1,0:T(8,128)(2,1)} %param.16) | copy-start | bytes 1966084
  295.8 508.6 %all-reduce.3.cloned.1.call-start = ((), (), s32[]{:S(2)}) async-start(), calls=%async_computation.10 | async-start | bytes 327680
  608.4 347.4 %reduce-scatter.11.cloned.1.call-start = ((), (), s32[]{:S(2)}) async-start(), calls=%async_computation.9 | async-start | bytes 1351680
  611.2 31.7 %all-to-all-start.2 = ((bf16[16,128,256]{2,1,0:T(8,128)(2,1)}), bf16[16,128,256]{2,1,0:T(8,128)(2,1)S(1)}, u32[]{:S(2)}, u32[]{:S(2)}) async-start(bf16[16,128,256]{2,1,0:T(8,128)(2,1)} %bitcast.19), calls=%async_computation.2 | async-start | bytes 2097152 | tf_op jit(solution)/shard_map/all_to_all | solution.py:213
  (4 other events, 6.1 us)
Sparse Core Ops, SparseCore 0:
  10.1 172.5 all-gather.1
  293.1 154.6 reduce-scatter.6
  450.8 155.6 reduce-scatter.8
  609.4 194.9 all-reduce.2
  807.3 148.4 reduce-scatter.10
where the time goes:
time: 981 us; the launch traced here: 965 us
  waiting for transfers between devices  787 us (80%)
  local copies, waits for them, and re-layouts  66.5 us (7%)
  matrix products  58.9 us (6%)
  starting transfers between devices  29.8 us (3%)
  between operations  15.4 us (2%)
    unnamed x7, waiting for transfers between devices  310 us
    reduce_scatter x1, waiting for transfers between devices, body(): lax.psum_scatter(value_part.astype(jnp.bfloat16), 'seq', scatter_dimensio...  157 us
    reduce_scatter x1, waiting for transfers between devices, body(): lax.psum_scatter(key_part.astype(jnp.bfloat16), 'seq', scatter_dimension=...  152 us
    all_gather x1, waiting for transfers between devices, body(): lax.all_gather(latents, 'seq', axis=0, tiled=True)  102 us
    all_to_all x1, waiting for transfers between devices, body(): lax.all_to_all(out_grad, 'head', split_axis=1, concat_axis=0, tiled=True)  28.3 us
    dynamic_slice x24, local copies, waits for them, and re-layouts, body(): grad_queries, grad_keys, grad_values = lax.map(attend, tile_inputs)  20.8 us
    all_to_all x1, waiting for transfers between devices, body(): lax.all_to_all(grad_queries.reshape(token_rows, local_width), 'head', spl...  19.8 us
  transfers between devices with their start and end apart: 8, of which 8 were waited for; matrix products, arithmetic and copies ran while one was open for 2% of the time, Pallas kernels for 0%

commit v1 on v0

v1 whole, which is shorter than its diff:
```python
import jax
import jax.numpy as jnp
from jax import lax
from jax.experimental import pallas as pl
from jax.experimental.pallas import tpu as pltpu
from jax.sharding import PartitionSpec as P

HD = 128
EPS = 1e-06
SCALE = HD ** (-0.5)
LOG2E = 1.4426950408889634
MESH = pl.DeviceIdType.MESH

NZ = 8
NL = 4
NY = 8
NX = 8
LAT = 64
LIST = 8
TILE = 512
TOK = 1024
OWN = 128
COLS = 256
VD = 1280
PAD = 48
SLOTS = 32
DEAD = 1 << 30

F32 = jnp.float32
BF16 = jnp.bfloat16


def dot(a, b, ca, cb):
    return lax.dot_general(a, b, (((ca,), (cb,)), ((), ())), preferred_element_type=F32)


class Place:
    def __init__(self):
        self.seq = lax.axis_index("seq")
        self.head = lax.axis_index("head")
        self.z = lax.rem(self.seq, NZ)
        self.yl = lax.div(self.seq, NZ)
        self.yh = lax.div(self.head, NX)
        self.xc = lax.rem(self.head, NX)
        self.y = self.yh * NL + self.yl

    def at_y(self, step):
        y = lax.rem(self.y + (step + NY), NY)
        return (lax.rem(y, NL) * NZ + self.z, lax.div(y, NL) * NX + self.xc)

    def at_z(self, step):
        z = lax.rem(self.z + (step + NZ), NZ)
        return (self.yl * NZ + z, self.head)

    def at_x(self, step):
        return (self.seq, self.yh * NX + lax.rem(self.xc + step, NX))

    def at_head(self, step):
        return (self.seq, lax.rem(self.head + step, 2 * NX))

    def at_low(self, step):
        return (lax.rem(self.yl + step, NL) * NZ + self.z, self.head)


def greet(partners):
    barrier = pltpu.get_barrier_semaphore()
    for partner in partners:
        pl.semaphore_signal(barrier, inc=1, device_id=partner, device_id_type=MESH)
    pl.semaphore_wait(barrier, len(partners))


def remote(src, dst, sends, recvs, sem, device):
    return pltpu.make_async_remote_copy(
        src_ref=src,
        dst_ref=dst,
        send_sem=sends.at[sem],
        recv_sem=recvs.at[sem],
        device_id=device,
        device_id_type=MESH,
    )


class GatherRing:
    def __init__(self, block, me, right, left, sends, recvs, base):
        self.block, self.me, self.targets = block, me, (right, left)
        self.sends, self.recvs, self.base = sends, recvs, base
        self.started = []

    def copy(self, way, step, shift):
        offset = (-step - shift) if way == 0 else (step + shift)
        ref = self.block(lax.rem(self.me + (offset + 8), 8), way if step == 3 else None)
        return remote(ref, ref, self.sends, self.recvs, self.base + way * 4 + step, self.targets[way])

    def start(self, step):
        for way in (0, 1):
            copy = self.copy(way, step, 0)
            copy.start()
            self.started.append(copy)

    def wait(self, step):
        for way in (0, 1):
            self.copy(way, step, 1).wait_recv()

    def finish(self):
        for copy in self.started:
            copy.wait_send()


class ReduceRing:
    def __init__(self, own, inbox, me, right, left, sends, recvs, base):
        self.own, self.inbox, self.me, self.targets = own, inbox, me, (right, left)
        self.sends, self.recvs, self.base = sends, recvs, base
        self.started = []

    def index(self, way, step):
        offset = 4 - step if way == 0 else step + 4
        return lax.rem(self.me + offset, 8)

    def send(self, way, step, src):
        copy = remote(
            src, self.inbox(way, step), self.sends, self.recvs, self.base + way * 4 + step, self.targets[way]
        )
        copy.start()
        self.started.append(copy)

    def arrive(self, way, step):
        ref = self.inbox(way, step)
        remote(ref, ref, self.sends, self.recvs, self.base + way * 4 + step, self.targets[way]).wait_recv()

    def start(self):
        for way in (0, 1):
            self.send(way, 0, self.own(self.index(way, 0), way))

    def step(self, step):
        for way in (0, 1):
            self.arrive(way, step - 1)
            index = self.index(way, step)
            here = self.inbox(way, step - 1)
            if step == 1:
                part = self.own(index, way)
                part[...] = (part[...].astype(F32) + here[...].astype(F32)).astype(BF16)
                self.send(way, 1, self.own(index, None))
            else:
                here[...] = (here[...].astype(F32) + self.own(index, None)[...].astype(F32)).astype(BF16)
                self.send(way, step, here)

    def total(self):
        for way in (0, 1):
            self.arrive(way, 3)
        return (
            self.own(self.me, None)[...].astype(F32)
            + self.inbox(0, 3)[...].astype(F32)
            + self.inbox(1, 3)[...].astype(F32)
        )

    def finish(self):
        for copy in self.started:
            copy.wait_send()


def halves(ref, size, half):
    return ref if half is None else ref.at[pl.ds(half * size, size)]


def gather_kernel(
    queries, out_grad, latents, key_weight, value_weight, key_gain,
    q_rows, g_rows, keys, values, raw_out,
    ring_send, ring_recv, swap_send, swap_recv, local_sem,
):
    me = Place()
    greet([me.at_y(1), me.at_y(-1), me.at_z(1), me.at_z(-1)] + [me.at_x(d) for d in range(1, NX)])

    flat = latents[...]
    raw = jnp.dot(flat, key_weight[...], preferred_element_type=F32)
    raw_out[...] = raw
    for h in range(2):
        part = raw[:, h * HD:(h + 1) * HD]
        inverse = lax.rsqrt(jnp.mean(part * part, axis=1, keepdims=True) + EPS)
        keys[me.y, me.z, :, h * HD:(h + 1) * HD] = (part * inverse * key_gain[...]).astype(BF16)
    values[me.z, me.y] = jnp.dot(flat, value_weight[...], preferred_element_type=F32).astype(BF16)

    half_row = LAT // 2
    key_z = GatherRing(
        lambda b, half: halves(keys.at[me.y, b], half_row, half),
        me.z, me.at_z(1), me.at_z(-1), ring_send, ring_recv, 0)
    value_y = GatherRing(
        lambda b, half: halves(values.at[me.z, b], half_row, half),
        me.y, me.at_y(1), me.at_y(-1), ring_send, ring_recv, 8)
    key_y = GatherRing(
        lambda b, half: halves(keys.at[b], NZ // 2, half),
        me.y, me.at_y(1), me.at_y(-1), ring_send, ring_recv, 16)
    value_z = GatherRing(
        lambda b, half: halves(values.at[b], NY // 2, half),
        me.z, me.at_z(1), me.at_z(-1), ring_send, ring_recv, 24)

    key_z.start(0)
    value_y.start(0)

    swaps = []
    own = []
    for d in range(NX):
        to = lax.rem(me.xc + d, NX)
        rows = pl.ds(pl.multiple_of(me.xc * OWN, OWN), OWN)
        for n, (src, dst) in enumerate(((queries, q_rows), (out_grad, g_rows))):
            for c in range(2):
                cols = pl.ds(pl.multiple_of(c * NX * COLS + to * COLS, COLS), COLS)
                if d == 0:
                    copy = pltpu.make_async_copy(src.at[:, cols], dst.at[c, rows], local_sem.at[n * 2 + c])
                    own.append(copy)
                else:
                    copy = remote(
                        src.at[:, cols], dst.at[c, rows], swap_send, swap_recv,
                        (d - 1) * 4 + n * 2 + c, me.at_x(d))
                    swaps.append(copy)
                copy.start()

    for step in range(4):
        for first in (key_z, value_y):
            first.wait(step)
            if step < 3:
                first.start(step + 1)
    key_y.start(0)
    value_z.start(0)
    for step in range(4):
        for second in (key_y, value_z):
            second.wait(step)
            if step < 3:
                second.start(step + 1)

    for d in range(1, NX):
        source = lax.rem(me.xc + (NX - d), NX)
        rows = pl.ds(pl.multiple_of(source * OWN, OWN), OWN)
        for n, dst in enumerate((q_rows, g_rows)):
            for c in range(2):
                place = dst.at[c, rows]
                remote(place, place, swap_send, swap_recv, (d - 1) * 4 + n * 2 + c, me.at_x(d)).wait_recv()
    for copy in own:
        copy.wait()
    for copy in swaps:
        copy.wait_send()
    for ring in (key_z, value_y, key_y, value_z):
        ring.finish()


def attend_kernel(
    entry_key, entry_value, entry_place, slot_entry, first_token, gate,
    q_rows, g_rows, keys, values, query_gain,
    grad_q, grad_keys, grad_values,
    key_tile, value_tile, key_sums, value_sums,
):
    gate_value = gate[0]
    gain = query_gain[...]
    for t in range(2):
        for c in range(2):
            key_sums[t, c, LIST] = jnp.zeros((LAT, COLS), F32)
            value_sums[t, c, LIST] = jnp.zeros((LAT, COLS), F32)

    half = 256
    for t in range(2):
        for c in range(2):
            for e in range(LIST):
                rows = slice(e * LAT, (e + 1) * LAT)
                key_tile[rows, :] = keys[c * SLOTS + entry_key[t, e]]
                value_tile[rows, :] = values[c * NL + entry_value[t, e]]
            for h in range(2):
                cols = slice(h * HD, (h + 1) * HD)
                kt = key_tile[:, cols]
                vt = value_tile[:, cols]
                kt_t = kt.T
                for part in range(2):
                    base = t * TILE + part * half
                    q = q_rows[c, base:base + half, cols].astype(F32)
                    g = g_rows[c, base:base + half, cols].astype(F32)
                    inverse = lax.rsqrt(jnp.mean(q * q, axis=1, keepdims=True) + EPS)
                    q_hat = (q * inverse * gain).astype(BF16)
                    ctx = (gate_value * g).astype(BF16)
                    scores = dot(kt, q_hat, 1, 1)
                    grad_probs = dot(vt, ctx, 1, 1)
                    token = first_token[0] + base + lax.broadcasted_iota(jnp.int32, (1, half), 1)
                    total = jnp.zeros((1, half), F32)
                    inner = jnp.zeros((1, half), F32)
                    dead = jnp.ones((1, half), F32)
                    exps = []
                    for e in range(LIST):
                        rows = slice(e * LAT, (e + 1) * LAT)
                        live = entry_place[t, e] < token
                        dead = jnp.where(live, 0.0, dead)
                        x = jnp.where(live, jnp.exp2(scores[rows] * (SCALE * LOG2E)), 0.0)
                        exps.append(x)
                        total = total + jnp.sum(x, axis=0, keepdims=True)
                        inner = inner + jnp.sum(x * grad_probs[rows], axis=0, keepdims=True)
                    norm = 1.0 / (total + dead)
                    inner = inner * norm
                    probs = []
                    grads = []
                    for e in range(LIST):
                        rows = slice(e * LAT, (e + 1) * LAT)
                        p = exps[e] * norm
                        probs.append(p.astype(BF16))
                        grads.append((p * (grad_probs[rows] - inner)).astype(BF16))
                    probs = jnp.concatenate(probs, axis=0)
                    grads = jnp.concatenate(grads, axis=0)
                    dk = dot(grads, q_hat, 1, 0) * SCALE
                    dv = dot(probs, ctx, 1, 0)
                    up = dot(kt_t, grads, 1, 0).T * SCALE * gain
                    row_inner = jnp.mean(up * q, axis=1, keepdims=True)
                    grad_q[c, base:base + half, cols] = (
                        inverse * (up - q * (inverse * inverse * row_inner))
                    ).astype(BF16)
                    for e in range(LIST):
                        rows = slice(e * LAT, (e + 1) * LAT)
                        if part == 0:
                            key_sums[t, c, e, :, cols] = dk[rows]
                            value_sums[t, c, e, :, cols] = dv[rows]
                        else:
                            key_sums[t, c, e, :, cols] += dk[rows]
                            value_sums[t, c, e, :, cols] += dv[rows]

    def one_slot(s, carry):
        first = slot_entry[0, s]
        second = slot_entry[1, s]
        z = lax.rem(s, NZ)
        low = lax.div(s, NZ)
        for c in range(2):
            grad_keys[c * NL + low, z] = (key_sums[0, c, first] + key_sums[1, c, second]).astype(BF16)
            grad_values[z, c * NL + low] = (value_sums[0, c, first] + value_sums[1, c, second]).astype(BF16)
        return carry

    lax.fori_loop(0, SLOTS, one_slot, 0)


def reduce_kernel(
    grad_q, grad_keys_in, grad_values_in, raw, key_gain, key_weight, value_weight, latents_t,
    out_queries, out_latents, out_key_weight, out_value_weight,
    grad_keys, grad_values, key_in, value_in, key_mid, value_mid, key_low, value_low,
    shares, shares_in, spread, wide, weights, weights_in, low_out, low_in,
    load_sem, ring_send, ring_recv, swap_send, swap_recv, own_sem, head_send, head_recv, low_send, low_recv,
):
    me = Place()
    load_keys = pltpu.make_async_copy(grad_keys_in, grad_keys, load_sem.at[0])
    load_values = pltpu.make_async_copy(grad_values_in, grad_values, load_sem.at[1])
    load_keys.start()
    load_values.start()
    greet(
        [me.at_y(1), me.at_y(-1), me.at_z(1), me.at_z(-1)]
        + [me.at_head(d) for d in range(1, 2 * NX)]
        + [me.at_x(d) for d in range(1, NX)]
        + [me.at_low(d) for d in range(1, NL)]
    )
    load_keys.wait()
    load_values.wait()

    def inbox(buffer, size):
        def place(way, step):
            ref = buffer.at[way, step]
            return ref.at[pl.ds(way * size, size)] if step == 0 else ref
        return place

    key_y = ReduceRing(
        lambda b, half: halves(grad_keys.at[b], NZ // 2, half), inbox(key_in, NZ // 2),
        me.y, me.at_y(1), me.at_y(-1), ring_send, ring_recv, 0)
    value_z = ReduceRing(
        lambda b, half: halves(grad_values.at[b], NY // 2, half), inbox(value_in, NY // 2),
        me.z, me.at_z(1), me.at_z(-1), ring_send, ring_recv, 8)
    key_z = ReduceRing(
        lambda b, half: halves(key_mid.at[b], LAT // 2, half), inbox(key_low, LAT // 2),
        me.z, me.at_z(1), me.at_z(-1), ring_send, ring_recv, 16)
    value_y = ReduceRing(
        lambda b, half: halves(value_mid.at[b], LAT // 2, half), inbox(value_low, LAT // 2),
        me.y, me.at_y(1), me.at_y(-1), ring_send, ring_recv, 24)

    key_y.start()
    value_z.start()

    swaps = []
    own = []
    cols_of = lambda c, place: pl.ds(pl.multiple_of(c * NX * COLS + place * COLS, COLS), COLS)
    for d in range(NX):
        to = lax.rem(me.xc + d, NX)
        rows = pl.ds(pl.multiple_of(to * OWN, OWN), OWN)
        for c in range(2):
            src = grad_q.at[c, rows]
            dst = out_queries.at[:, cols_of(c, me.xc)]
            if d == 0:
                copy = pltpu.make_async_copy(src, dst, own_sem.at[c])
                own.append(copy)
            else:
                copy = remote(src, dst, swap_send, swap_recv, (d - 1) * 2 + c, me.at_x(d))
                swaps.append(copy)
            copy.start()

    for step in range(1, 4):
        key_y.step(step)
        value_z.step(step)
    key_mid[...] = key_y.total().astype(BF16)
    key_z.start()
    value_mid[...] = value_z.total().astype(BF16)
    value_y.start()
    for step in range(1, 4):
        key_z.step(step)
        value_y.step(step)
    key_sum = key_z.total()
    value_sum = value_y.total()

    parts = []
    for h in range(2):
        cols = slice(h * HD, (h + 1) * HD)
        rows = raw[:, cols]
        inverse = lax.rsqrt(jnp.mean(rows * rows, axis=1, keepdims=True) + EPS)
        up = key_sum[:, cols] * key_gain[...]
        row_inner = jnp.mean(up * rows, axis=1, keepdims=True)
        parts.append((inverse * (up - rows * (inverse * inverse * row_inner))).astype(BF16))
    raw_grad = jnp.concatenate(parts, axis=1)
    value_grad = value_sum.astype(BF16)

    lat = latents_t[...]
    for c, grad in enumerate((raw_grad, value_grad)):
        share = jnp.dot(lat, grad, preferred_element_type=F32).astype(BF16)
        weights[:, :, :, c * COLS:(c + 1) * COLS] = share.reshape(NZ, NL, PAD, COLS)
    weight_z = ReduceRing(
        lambda b, half: halves(weights.at[b], NL // 2, half), inbox(weights_in, NL // 2),
        me.z, me.at_z(1), me.at_z(-1), ring_send, ring_recv, 32)
    weight_z.start()

    wide[...] = dot(raw_grad, key_weight[...], 1, 1) + dot(value_grad, value_weight[...], 1, 1)
    spread[...] = jnp.zeros_like(spread)
    for d in range(2 * NX):
        for n in range(VD // HD):
            spread[d, 4 * n:4 * n + 4, :] = wide[4 * d:4 * d + 4, n * HD:(n + 1) * HD]
    shares[...] = spread[...].astype(BF16)
    head_copies = []
    for d in range(1, 2 * NX):
        copy = remote(
            shares.at[lax.rem(me.head + d, 2 * NX)], shares_in.at[d], head_send, head_recv, d, me.at_head(d))
        copy.start()
        head_copies.append(copy)

    for step in range(1, 4):
        weight_z.step(step)
    low_out[...] = weight_z.total().astype(BF16)
    low_copies = []
    for d in range(1, NL):
        copy = remote(low_out.at[lax.rem(me.yl + d, NL)], low_in.at[d], low_send, low_recv, d, me.at_low(d))
        copy.start()
        low_copies.append(copy)

    total = shares[me.head].astype(F32)
    for d in range(1, 2 * NX):
        place = shares_in.at[d]
        remote(place, place, head_send, head_recv, d, me.at_head(d)).wait_recv()
        total = total + place[...].astype(F32)
    spread[0] = total
    for n in range(VD // HD):
        wide[0:4, n * HD:(n + 1) * HD] = spread[0, 4 * n:4 * n + 4, :]
    out_latents[...] = wide[0:4, :].astype(BF16)

    total = low_out[me.yl].astype(F32)
    for d in range(1, NL):
        place = low_in.at[d]
        remote(place, place, low_send, low_recv, d, me.at_low(d)).wait_recv()
        total = total + place[...].astype(F32)
    out_key_weight[...] = total[0:40, 0:COLS]
    out_value_weight[...] = total[0:40, COLS:]

    for d in range(1, NX):
        source = lax.rem(me.xc + (NX - d), NX)
        for c in range(2):
            place = out_queries.at[:, cols_of(c, source)]
            remote(place, place, swap_send, swap_recv, (d - 1) * 2 + c, me.at_x(d)).wait_recv()
    for copy in own:
        copy.wait()
    for copy in swaps + head_copies + low_copies:
        copy.wait_send()
    for ring in (key_y, value_z, key_z, value_y, weight_z):
        ring.finish()


VMEM = pl.BlockSpec(memory_space=pltpu.VMEM)
SMEM = pl.BlockSpec(memory_space=pltpu.SMEM)
HBM = pl.BlockSpec(memory_space=pl.ANY)
LIMIT = 48 * 1024 * 1024
DMA = pltpu.SemaphoreType.DMA


def struct(shape, dtype):
    return jax.ShapeDtypeStruct(shape, dtype)


def body(
    queries,
    out_grad,
    latents,
    key_weight,
    value_weight,
    query_gain,
    key_gain,
    gate_alpha,
    media_slot,
    media_position,
    tile_list,
):
    seq = lax.axis_index("seq")
    high = lax.div(lax.axis_index("head"), NX)
    flat = latents.reshape(LAT, VD)
    gain_q = query_gain.reshape(1, HD)
    gain_k = key_gain.reshape(1, HD)

    q_rows, g_rows, keys, values, raw = pl.pallas_call(
        gather_kernel,
        out_shape=(
            struct((2, TOK, COLS), BF16),
            struct((2, TOK, COLS), BF16),
            struct((NY, NZ, LAT, COLS), BF16),
            struct((NZ, NY, LAT, COLS), BF16),
            struct((LAT, COLS), F32),
        ),
        in_specs=[HBM, HBM, VMEM, VMEM, VMEM, VMEM],
        out_specs=(HBM, HBM, VMEM, VMEM, VMEM),
        scratch_shapes=[DMA((32,)), DMA((32,)), DMA((28,)), DMA((28,)), DMA((4,))],
        compiler_params=pltpu.CompilerParams(collective_id=0, has_side_effects=True, vmem_limit_bytes=LIMIT),
        name="gather",
    )(queries, out_grad, flat, key_weight, value_weight, gain_k)

    lists = lax.dynamic_slice_in_dim(tile_list, high * 2, 2, 0)
    image_range = jnp.arange(SLOTS, dtype=jnp.int32)
    live = lists >= 0
    matches = lists[:, :, None] == image_range
    slot = jnp.sum(jnp.where(matches, media_slot, 0), axis=2)
    place = jnp.where(live, jnp.sum(jnp.where(matches, media_position, 0), axis=2), DEAD)
    entry_value = lax.rem(slot, NZ) * NY + lax.div(slot, NZ)
    hit = live[:, :, None] & (slot[:, :, None] == image_range)
    entry_range = jnp.arange(LIST, dtype=jnp.int32)[None, :, None]
    slot_entry = LIST - jnp.sum(jnp.where(hit, LIST - entry_range, 0), axis=1)
    first_token = (seq * (2 * TOK) + high * TOK).reshape(1).astype(jnp.int32)

    grad_q, grad_keys, grad_values = pl.pallas_call(
        attend_kernel,
        out_shape=(
            struct((2, TOK, COLS), BF16),
            struct((NY, NZ, LAT, COLS), BF16),
            struct((NZ, NY, LAT, COLS), BF16),
        ),
        in_specs=[SMEM] * 6 + [VMEM] * 5,
        out_specs=(VMEM, VMEM, VMEM),
        scratch_shapes=[
            pltpu.VMEM((LIST * LAT, COLS), BF16),
            pltpu.VMEM((LIST * LAT, COLS), BF16),
            pltpu.VMEM((2, 2, LIST + 1, LAT, COLS), F32),
            pltpu.VMEM((2, 2, LIST + 1, LAT, COLS), F32),
        ],
        compiler_params=pltpu.CompilerParams(vmem_limit_bytes=LIMIT),
        name="attend",
    )(
        slot, entry_value, place, slot_entry, first_token, jnp.tanh(gate_alpha),
        q_rows, g_rows, keys.reshape(2 * SLOTS, LAT, COLS), values.reshape(2 * SLOTS, LAT, COLS), gain_q,
    )

    latents_t = flat.T.reshape(NL, NZ, VD // SLOTS, LAT).transpose(1, 0, 2, 3)
    latents_t = jnp.pad(latents_t, ((0, 0), (0, 0), (0, PAD - VD // SLOTS), (0, 0)))
    latents_t = latents_t.reshape(NZ * NL * PAD, LAT)

    block = (LAT, COLS)
    return pl.pallas_call(
        reduce_kernel,
        out_shape=(
            struct((OWN, 2 * NX * COLS), BF16),
            struct((4, VD), BF16),
            struct((VD // SLOTS, COLS), F32),
            struct((VD // SLOTS, COLS), F32),
        ),
        in_specs=[HBM, HBM, HBM] + [VMEM] * 5,
        out_specs=(HBM, VMEM, VMEM, VMEM),
        scratch_shapes=[
            pltpu.VMEM((NY, NZ) + block, BF16),
            pltpu.VMEM((NZ, NY) + block, BF16),
            pltpu.VMEM((2, 4, NZ) + block, BF16),
            pltpu.VMEM((2, 4, NY) + block, BF16),
            pltpu.VMEM((NZ,) + block, BF16),
            pltpu.VMEM((NY,) + block, BF16),
            pltpu.VMEM((2, 4) + block, BF16),
            pltpu.VMEM((2, 4) + block, BF16),
            pltpu.VMEM((2 * NX, PAD, HD), BF16),
            pltpu.VMEM((2 * NX, PAD, HD), BF16),
            pltpu.VMEM((2 * NX, PAD, HD), F32),
            pltpu.VMEM((LAT, VD), F32),
            pltpu.VMEM((NZ, NL, PAD, 2 * COLS), BF16),
            pltpu.VMEM((2, 4, NL, PAD, 2 * COLS), BF16),
            pltpu.VMEM((NL, PAD, 2 * COLS), BF16),
            pltpu.VMEM((NL, PAD, 2 * COLS), BF16),
            DMA((2,)),
            DMA((40,)), DMA((40,)), DMA((14,)), DMA((14,)), DMA((2,)),
            DMA((16,)), DMA((16,)), DMA((4,)), DMA((4,)),
        ],
        compiler_params=pltpu.CompilerParams(collective_id=1, has_side_effects=True, vmem_limit_bytes=LIMIT),
        name="reduce",
    )(grad_q, grad_keys, grad_values, raw, gain_k, key_weight, value_weight, latents_t)


def solution(mesh):
    in_specs = (
        P(("seq", "head"), None),
        P(("seq", "head"), None),
        P("seq", None, None),
        P(None, "head"),
        P(None, "head"),
        P(),
        P(),
        P(),
        P(),
        P(),
        P("seq", None),
    )
    out_specs = (
        P(("seq", "head"), None),
        P("seq", "head", None),
        P("seq", "head"),
        P("seq", "head"),
    )

    def run(*args):
        query_grad, latent_grad, key_weight_grad, value_weight_grad = body(*args)
        return (query_grad, latent_grad.reshape(1, 4, VD), key_weight_grad, value_weight_grad)

    return jax.shard_map(run, mesh=mesh, in_specs=in_specs, out_specs=out_specs, check_vma=False)
```

time: 981 us -> 164 us (0.17); the launches traced: 965 us -> 163 us
  waiting for transfers between devices: 787 us -> 0 us
  Pallas kernels: 0 us -> 145 us
  matrix products: 58.9 us -> 0 us
  local copies, waits for them, and re-layouts: 66.5 us -> 14.9 us
  starting transfers between devices: 29.8 us -> 0 us
  between operations: 15.4 us -> 1.44 us
    unnamed x7 -> x0, waiting for transfers between devices: 310 us -> none
    reduce_scatter x2 -> x0, waiting for transfers between devices: 309 us -> none  [the longest x1 157 us: body(): lax.psum_scatter(value_part.astype(jnp.bfloat16), 'seq', scatter_dimensio...]
    pallas_call x0 -> x3, Pallas kernels: none -> 145 us  [the longest x1 75.1 us: body(): pl.pallas_call(reduce_kernel, out_shape=(struct((OWN, 2 * NX * COLS), BF1...]
    all_gather x1 -> x0, waiting for transfers between devices: 102 us -> none  [body(): lax.all_gather(latents, 'seq', axis=0, tiled=True)]
    all_to_all x3 -> x0, waiting for transfers between devices: 64.9 us -> none  [the longest x1 28.3 us: body(): lax.all_to_all(out_grad, 'head', split_axis=1, concat_axis=0, tiled=True)]
    dot_general x30 -> x0, matrix products: 58.9 us -> none  [the longest x4 12.3 us: attend(): jnp.einsum('hqk,khd->qhd', grad_scores, key_tile, preferred_element_type=...]
    all_to_all x3 -> x0, starting transfers between devices: 29.6 us -> none  [the longest x1 9.95 us: body(): lax.all_to_all(grad_queries.reshape(token_rows, local_width), 'head', spl...]
    dynamic_slice x24 -> x1, local copies, waits for them, and re-layouts: 20.8 us -> 0.69 us  [body(): lists = lax.dynamic_slice_in_dim(tile_list, high * 2, 2, 0)]
  transfers between devices with their start and end apart: 8 -> 0, of which waited for: 8 -> 0; matrix products, arithmetic and copies ran while one was open for 2% -> 0% of each run, Pallas kernels for 0% -> 0%
where the time goes in v1:
time: 164 us; the launch traced here: 163 us
  Pallas kernels  145 us (88%)
  local copies, waits for them, and re-layouts  14.9 us (9%)
  other arithmetic  1.68 us (1%)
    pallas_call x1, Pallas kernels, body(): pl.pallas_call(reduce_kernel, out_shape=(struct((OWN, 2 * NX * COLS), BF1...  75.1 us
    pallas_call x1, Pallas kernels, body(): pl.pallas_call(gather_kernel, out_shape=(struct((2, TOK, COLS), BF16), st...  56 us
    pallas_call x1, Pallas kernels, body(): pl.pallas_call(attend_kernel, out_shape=(struct((2, TOK, COLS), BF16), st...  14 us
    unnamed x29, local copies, waits for them, and re-layouts  12.2 us

profile of v1, /device:TPU:56, one launch (start us, length us, event | category | flops | bytes accessed | tf_op | source)
XLA Modules:
  0.0 163.1 jit_solution(18154112313719122584)
XLA Ops:
  0.7 0.7 constant_dynamic-slice_fusion
  1.3 0.9 select_reduce_fusion.1
  2.2 0.7 broadcast_select_fusion
  2.9 0.1 select_reduce_fusion
  3.0 0.0 copy-start
  3.0 1.1 copy-done
  4.1 1.1 copy-done.2
  5.2 1.2 copy-done.4
  6.4 1.2 copy-done.5
  7.7 0.9 copy-done.8
  8.6 0.7 copy-done.9
  9.2 56.0 %gather.1 = (bf16[2,1024,256]{2,1,0:T(8,128)(2,1)S(1)}, bf16[2,1024,256]{2,1,0:T(8,128)(2,1)S(1)}, bf16[8,8,64,256]{3,2,1,0:T(8,128)(2,1)}, bf16[8,8,64,256]{3,2,1,0:T(8,128)(2,1)}, f32[64,256]{1,0:T(8,128)S(1)}) custom-call(bf16[128,4096]{1,0:T(8,128)(2,1)S(1)} %copy-done.4, bf16[128,4096]{1,0:T(8,128)(2,1)S(1)} %copy-done.5, ...), custom_call_target="tpu_custom_call" | custom-call | tf_op jit(solution)/shard_map/gather/pallas_call | solution.py:508
  66.0 0.0 copy-start.10
  66.0 14.0 %attend.1 = (bf16[2,1024,256]{2,1,0:T(8,128)(2,1)S(1)}, bf16[8,8,64,256]{3,2,1,0:T(8,128)(2,1)S(1)}, bf16[8,8,64,256]{3,2,1,0:T(8,128)(2,1)}) custom-call(s32[2,8]{1,0:T(2,128)S(1)} %get-tuple-element.29.entry_key, s32[2,8]{1,0:T(2,128)S(1)} %get-tuple-element.32.entry_value, s32[2,8]{1,0:T(2,128)S(1)} %get-tuple-element.30.entry_place, ...), custom_call_target="tpu_custom_call" | custom-call | tf_op jit(solution)/shard_map/attend/pallas_call | solution.py:536
  79.9 1.0 copy-done.6
  80.9 1.9 %copy.18 = bf16[1280,64]{1,0:T(8,128)(2,1)} copy(bf16[1280,64]{0,1:T(8,128)(2,1)} %bitcast.14) | data formatting | bytes 327680 | tf_op jit(solution)/shard_map/transpose | solution.py:558
  82.8 1.0 copy.20
  83.8 0.1 pad.4.clone
  84.0 1.2 copy-done.7
  85.2 75.1 %reduce.1 = (bf16[128,4096]{1,0:T(8,128)(2,1)S(1)}, bf16[4,1280]{1,0:T(4,128)(2,1)S(1)}, f32[40,256]{1,0:T(8,128)S(1)}, f32[40,256]{1,0:T(8,128)S(1)}) custom-call(bf16[2,1024,256]{2,1,0:T(8,128)(2,1)S(1)} %copy-done.7, bf16[8,8,64,256]{3,2,1,0:T(8,128)(2,1)S(1)} %get-tuple-element.21.grad_keys_in, bf16[8,8,64,256]{3,2,1,0:T(8,128)(2,1)} %get-tuple-element.22.grad_values_in, ...), custom_call_target="tpu_custom_call" | custom-call | tf_op jit(solution)/shard_map/reduce/pallas_call | solution.py:563
  160.3 1.0 copy.26
  161.3 0.6 copy.27
  161.9 0.6 copy.28
  162.5 0.6 copy.29
  (16 shorter events, 0.0 us)
Async XLA Ops:
  0.6 65.3 %copy-start.11 = (f32[128]{0:T(128)S(1)}, f32[128]{0:T(128)}, u32[]{:S(2)}) copy-start(f32[128]{0:T(128)} %param.16) | copy-start | bytes 1540
  3.0 1.1 copy-start
  4.1 1.1 copy-start.2
  5.2 1.2 copy-start.4
  6.4 1.2 copy-start.5
  7.7 0.9 copy-start.8
  8.6 0.7 copy-start.9
  66.0 17.9 %copy-start.10 = (f32[128]{0:T(128)S(1)}, f32[128]{0:T(128)}, u32[]{:S(2)}) copy-start(f32[128]{0:T(128)} %param.17) | copy-start | bytes 1540
  79.9 1.0 copy-start.6
  80.9 3.0 %copy-start.1 = (bf16[1280,256]{1,0:T(8,128)(2,1)S(1)}, bf16[1280,256]{1,0:T(8,128)(2,1)}, u32[]{:S(2)}) copy-start(bf16[1280,256]{1,0:T(8,128)(2,1)} %key_weight.3) | copy-start | bytes 1966084
  80.9 3.0 %copy-start.3 = (bf16[1280,256]{1,0:T(8,128)(2,1)S(1)}, bf16[1280,256]{1,0:T(8,128)(2,1)}, u32[]{:S(2)}) copy-start(bf16[1280,256]{1,0:T(8,128)(2,1)} %value_weight.3) | copy-start | bytes 1966084
  84.0 1.2 copy-start.7

commit v2 on v0

v2 whole, which is shorter than its diff:
```python
import jax
import jax.numpy as jnp
from jax import lax
from jax.experimental import pallas as pl
from jax.experimental.pallas import tpu as pltpu
from jax.sharding import PartitionSpec as P

HD = 128
EPS = 1e-06
SCALE = HD ** (-0.5)
LOG2E = 1.4426950408889634
MESH = pl.DeviceIdType.MESH

NZ = 8
NL = 4
NY = 8
NX = 8
LAT = 64
LIST = 8
TILE = 512
TOK = 1024
OWN = 128
COLS = 256
VD = 1280
PAD = 48
SLOTS = 32
DEAD = 1 << 30

F32 = jnp.float32
BF16 = jnp.bfloat16


def dot(a, b, ca, cb):
    return lax.dot_general(a, b, (((ca,), (cb,)), ((), ())), preferred_element_type=F32)


class Place:
    def __init__(self):
        self.seq = lax.axis_index("seq")
        self.head = lax.axis_index("head")
        self.z = lax.rem(self.seq, NZ)
        self.yl = lax.div(self.seq, NZ)
        self.yh = lax.div(self.head, NX)
        self.xc = lax.rem(self.head, NX)
        self.y = self.yh * NL + self.yl

    def at_y(self, step):
        y = lax.rem(self.y + (step + NY), NY)
        return (lax.rem(y, NL) * NZ + self.z, lax.div(y, NL) * NX + self.xc)

    def at_z(self, step):
        z = lax.rem(self.z + (step + NZ), NZ)
        return (self.yl * NZ + z, self.head)

    def at_x(self, step):
        return (self.seq, self.yh * NX + lax.rem(self.xc + step, NX))

    def at_head(self, step):
        return (self.seq, lax.rem(self.head + step, 2 * NX))

    def at_low(self, step):
        return (lax.rem(self.yl + step, NL) * NZ + self.z, self.head)


def greet(partners):
    barrier = pltpu.get_barrier_semaphore()
    for partner in partners:
        pl.semaphore_signal(barrier, inc=1, device_id=partner, device_id_type=MESH)
    pl.semaphore_wait(barrier, len(partners))


def remote(src, dst, sends, recvs, sem, device):
    return pltpu.make_async_remote_copy(
        src_ref=src,
        dst_ref=dst,
        send_sem=sends.at[sem],
        recv_sem=recvs.at[sem],
        device_id=device,
        device_id_type=MESH,
    )


class GatherRing:
    def __init__(self, block, me, right, left, sends, recvs, base):
        self.block, self.me, self.targets = block, me, (right, left)
        self.sends, self.recvs, self.base = sends, recvs, base
        self.started = []

    def copy(self, way, step, shift):
        offset = (-step - shift) if way == 0 else (step + shift)
        ref = self.block(lax.rem(self.me + (offset + 8), 8), way if step == 3 else None)
        return remote(ref, ref, self.sends, self.recvs, self.base + way * 4 + step, self.targets[way])

    def start(self, step):
        for way in (0, 1):
            copy = self.copy(way, step, 0)
            copy.start()
            self.started.append(copy)

    def wait(self, step):
        for way in (0, 1):
            self.copy(way, step, 1).wait_recv()

    def finish(self):
        for copy in self.started:
            copy.wait_send()


class ReduceRing:
    def __init__(self, own, inbox, me, right, left, sends, recvs, base):
        self.own, self.inbox, self.me, self.targets = own, inbox, me, (right, left)
        self.sends, self.recvs, self.base = sends, recvs, base
        self.started = []

    def index(self, way, step):
        offset = 4 - step if way == 0 else step + 4
        return lax.rem(self.me + offset, 8)

    def send(self, way, step, src):
        copy = remote(
            src, self.inbox(way, step), self.sends, self.recvs, self.base + way * 4 + step, self.targets[way]
        )
        copy.start()
        self.started.append(copy)

    def arrive(self, way, step):
        ref = self.inbox(way, step)
        remote(ref, ref, self.sends, self.recvs, self.base + way * 4 + step, self.targets[way]).wait_recv()

    def start(self):
        for way in (0, 1):
            self.send(way, 0, self.own(self.index(way, 0), way))

    def step(self, step):
        for way in (0, 1):
            self.arrive(way, step - 1)
            index = self.index(way, step)
            here = self.inbox(way, step - 1)
            if step == 1:
                part = self.own(index, way)
                part[...] = (part[...].astype(F32) + here[...].astype(F32)).astype(BF16)
                self.send(way, 1, self.own(index, None))
            else:
                here[...] = (here[...].astype(F32) + self.own(index, None)[...].astype(F32)).astype(BF16)
                self.send(way, step, here)

    def total(self):
        for way in (0, 1):
            self.arrive(way, 3)
        return (
            self.own(self.me, None)[...].astype(F32)
            + self.inbox(0, 3)[...].astype(F32)
            + self.inbox(1, 3)[...].astype(F32)
        )

    def finish(self):
        for copy in self.started:
            copy.wait_send()


def halves(ref, size, half):
    return ref if half is None else ref.at[pl.ds(half * size, size)]


def scratch(*shape, dtype=BF16):
    return pltpu.VMEM(shape, dtype)


PIECE = dict(
    keys=scratch(NY, NZ, LAT, HD),
    values=scratch(NZ, NY, LAT, HD),
    q_rows=scratch(2, TOK, HD),
    g_rows=scratch(2, TOK, HD),
    grad_q=scratch(2, TOK, HD),
    grad_keys=scratch(NY, NZ, LAT, HD),
    grad_values=scratch(NZ, NY, LAT, HD),
    key_in=scratch(2, 4, NZ, LAT, HD),
    value_in=scratch(2, 4, NY, LAT, HD),
    key_mid=scratch(NZ, LAT, HD),
    value_mid=scratch(NY, LAT, HD),
    key_low=scratch(2, 4, LAT, HD),
    value_low=scratch(2, 4, LAT, HD),
    weights=scratch(NZ, NL, PAD, 2 * HD),
    weights_in=scratch(2, 4, NL, PAD, 2 * HD),
    low_out=scratch(NL, PAD, 2 * HD),
    low_in=scratch(NL, PAD, 2 * HD),
    ring_send=pltpu.SemaphoreType.DMA((72,)),
    ring_recv=pltpu.SemaphoreType.DMA((72,)),
    swap_send=pltpu.SemaphoreType.DMA((28,)),
    swap_recv=pltpu.SemaphoreType.DMA((28,)),
    swap_own=pltpu.SemaphoreType.DMA((4,)),
    back_send=pltpu.SemaphoreType.DMA((14,)),
    back_recv=pltpu.SemaphoreType.DMA((14,)),
    back_own=pltpu.SemaphoreType.DMA((2,)),
    low_send=pltpu.SemaphoreType.DMA((4,)),
    low_recv=pltpu.SemaphoreType.DMA((4,)),
)
SHARED = dict(
    latents=scratch(LAT, VD),
    key_weight=scratch(VD, COLS),
    value_weight=scratch(VD, COLS),
    raw=scratch(LAT, COLS, dtype=F32),
    key_tile=scratch(LIST * LAT, HD),
    value_tile=scratch(LIST * LAT, HD),
    key_sums=scratch(2, 2, LIST + 1, LAT, HD, dtype=F32),
    value_sums=scratch(2, 2, LIST + 1, LAT, HD, dtype=F32),
    shares=scratch(2 * NX, PAD, HD),
    shares_in=scratch(2 * NX, PAD, HD),
    spread=scratch(2 * NX, PAD, HD, dtype=F32),
    wide=scratch(LAT, VD, dtype=F32),
    load_sem=pltpu.SemaphoreType.DMA((3,)),
    head_send=pltpu.SemaphoreType.DMA((16,)),
    head_recv=pltpu.SemaphoreType.DMA((16,)),
)


class Refs:
    def __init__(self, names, refs):
        self.__dict__.update(zip(names, refs))


def inbox(buffer, size):
    def place(way, step):
        ref = buffer.at[way, step]
        return ref.at[pl.ds(way * size, size)] if step == 0 else ref

    return place


def gather_rings(me, p):
    y, z = (me.at_y(1), me.at_y(-1)), (me.at_z(1), me.at_z(-1))
    sems = (p.ring_send, p.ring_recv)
    first = (
        GatherRing(lambda b, half: halves(p.keys.at[me.y, b], LAT // 2, half), me.z, *z, *sems, 0),
        GatherRing(lambda b, half: halves(p.values.at[me.z, b], LAT // 2, half), me.y, *y, *sems, 8),
    )
    second = (
        GatherRing(lambda b, half: halves(p.keys.at[b], NZ // 2, half), me.y, *y, *sems, 16),
        GatherRing(lambda b, half: halves(p.values.at[b], NY // 2, half), me.z, *z, *sems, 24),
    )
    return first, second


def reduce_rings(me, p):
    y, z = (me.at_y(1), me.at_y(-1)), (me.at_z(1), me.at_z(-1))
    sems = (p.ring_send, p.ring_recv)
    key_y = ReduceRing(
        lambda b, half: halves(p.grad_keys.at[b], NZ // 2, half), inbox(p.key_in, NZ // 2), me.y, *y, *sems, 32)
    value_z = ReduceRing(
        lambda b, half: halves(p.grad_values.at[b], NY // 2, half), inbox(p.value_in, NY // 2), me.z, *z, *sems, 40)
    key_z = ReduceRing(
        lambda b, half: halves(p.key_mid.at[b], LAT // 2, half), inbox(p.key_low, LAT // 2), me.z, *z, *sems, 48)
    value_y = ReduceRing(
        lambda b, half: halves(p.value_mid.at[b], LAT // 2, half), inbox(p.value_low, LAT // 2), me.y, *y, *sems, 56)
    weight_z = ReduceRing(
        lambda b, half: halves(p.weights.at[b], NL // 2, half), inbox(p.weights_in, NL // 2), me.z, *z, *sems, 64)
    return key_y, value_z, key_z, value_y, weight_z


def columns(c, place, h):
    return pl.ds(pl.multiple_of((c * NX + place) * COLS + h * HD, HD), HD)


def rows_of(place):
    return pl.ds(pl.multiple_of(place * OWN, OWN), OWN)


class Swap:
    def __init__(self, me, p, h, queries, out_grad):
        self.me, self.p = me, p
        self.sent, self.own = [], []
        for d in range(NX):
            to = lax.rem(me.xc + d, NX)
            for n, (src, dst) in enumerate(((queries, p.q_rows), (out_grad, p.g_rows))):
                for c in range(2):
                    src_ref = src.at[:, columns(c, to, h)]
                    dst_ref = dst.at[c, rows_of(me.xc)]
                    if d == 0:
                        copy = pltpu.make_async_copy(src_ref, dst_ref, p.swap_own.at[n * 2 + c])
                        self.own.append(copy)
                    else:
                        sem = (d - 1) * 4 + n * 2 + c
                        copy = remote(src_ref, dst_ref, p.swap_send, p.swap_recv, sem, me.at_x(d))
                        self.sent.append(copy)
                    copy.start()

    def wait(self):
        me, p = self.me, self.p
        for d in range(1, NX):
            source = lax.rem(me.xc + (NX - d), NX)
            for n, dst in enumerate((p.q_rows, p.g_rows)):
                for c in range(2):
                    ref = dst.at[c, rows_of(source)]
                    sem = (d - 1) * 4 + n * 2 + c
                    remote(ref, ref, p.swap_send, p.swap_recv, sem, me.at_x(d)).wait_recv()
        for copy in self.own:
            copy.wait()

    def finish(self):
        for copy in self.sent:
            copy.wait_send()


class SwapBack:
    def __init__(self, me, p, h, out):
        self.me, self.p, self.h, self.out = me, p, h, out
        self.sent, self.own = [], []
        for d in range(NX):
            to = lax.rem(me.xc + d, NX)
            for c in range(2):
                src_ref = p.grad_q.at[c, rows_of(to)]
                dst_ref = out.at[:, columns(c, me.xc, h)]
                if d == 0:
                    copy = pltpu.make_async_copy(src_ref, dst_ref, p.back_own.at[c])
                    self.own.append(copy)
                else:
                    copy = remote(src_ref, dst_ref, p.back_send, p.back_recv, (d - 1) * 2 + c, me.at_x(d))
                    self.sent.append(copy)
                copy.start()

    def finish(self):
        me, p = self.me, self.p
        for d in range(1, NX):
            source = lax.rem(me.xc + (NX - d), NX)
            for c in range(2):
                ref = self.out.at[:, columns(c, source, self.h)]
                remote(ref, ref, p.back_send, p.back_recv, (d - 1) * 2 + c, me.at_x(d)).wait_recv()
        for copy in self.own:
            copy.wait()
        for copy in self.sent:
            copy.wait_send()


def attend(me, p, s, t, c, entries, gate, gain):
    for e in range(LIST):
        rows = slice(e * LAT, (e + 1) * LAT)
        slot = entries[t][e][0]
        s.key_tile[rows, :] = p.keys[c * NL + lax.div(slot, NZ), lax.rem(slot, NZ)]
        s.value_tile[rows, :] = p.values[lax.rem(slot, NZ), c * NL + lax.div(slot, NZ)]
    kt = s.key_tile[...]
    vt = s.value_tile[...]
    base = t * TILE
    q = p.q_rows[c, base:base + TILE, :].astype(F32)
    g = p.g_rows[c, base:base + TILE, :].astype(F32)
    inverse = lax.rsqrt(jnp.mean(q * q, axis=1, keepdims=True) + EPS)
    q_hat = (q * inverse * gain).astype(BF16)
    ctx = (gate * g).astype(BF16)
    scores = dot(kt, q_hat, 1, 1)
    grad_probs = dot(vt, ctx, 1, 1)
    token = me.seq * (2 * TOK) + me.yh * TOK + base + lax.broadcasted_iota(jnp.int32, (1, TILE), 1)
    total = jnp.zeros((1, TILE), F32)
    inner = jnp.zeros((1, TILE), F32)
    dead = jnp.ones((1, TILE), F32)
    exps = []
    for e in range(LIST):
        rows = slice(e * LAT, (e + 1) * LAT)
        live = entries[t][e][1] < token
        dead = jnp.where(live, 0.0, dead)
        x = jnp.where(live, jnp.exp2(scores[rows] * (SCALE * LOG2E)), 0.0)
        exps.append(x)
        total = total + jnp.sum(x, axis=0, keepdims=True)
        inner = inner + jnp.sum(x * grad_probs[rows], axis=0, keepdims=True)
    norm = 1.0 / (total + dead)
    inner = inner * norm
    probs = []
    grads = []
    for e in range(LIST):
        rows = slice(e * LAT, (e + 1) * LAT)
        prob = exps[e] * norm
        probs.append(prob.astype(BF16))
        grads.append((prob * (grad_probs[rows] - inner)).astype(BF16))
    probs = jnp.concatenate(probs, axis=0)
    grads = jnp.concatenate(grads, axis=0)
    s.key_sums[t, c, 0:LIST] = (dot(grads, q_hat, 1, 0) * SCALE).reshape(LIST, LAT, HD)
    s.value_sums[t, c, 0:LIST] = dot(probs, ctx, 1, 0).reshape(LIST, LAT, HD)
    up = dot(kt.T, grads, 1, 0).T * SCALE * gain
    row_inner = jnp.mean(up * q, axis=1, keepdims=True)
    p.grad_q[c, base:base + TILE, :] = (inverse * (up - q * (inverse * inverse * row_inner))).astype(BF16)


def to_slots(p, s, entries):
    def one_slot(slot, carry):
        z = lax.rem(slot, NZ)
        low = lax.div(slot, NZ)
        place = []
        for t in range(2):
            found = jnp.int32(LIST)
            for e in range(LIST):
                found = jnp.where(entries[t][e][2] == slot, e, found)
            place.append(found)
        for c in range(2):
            p.grad_keys[c * NL + low, z] = (
                s.key_sums[0, c, place[0]] + s.key_sums[1, c, place[1]]).astype(BF16)
            p.grad_values[z, c * NL + low] = (
                s.value_sums[0, c, place[0]] + s.value_sums[1, c, place[1]]).astype(BF16)
        return carry

    lax.fori_loop(0, SLOTS, one_slot, 0)


def kernel(
    tile_list, media_slot, media_position, gate_alpha,
    queries, out_grad, latents, key_weight, value_weight, query_gain, key_gain,
    out_queries, out_latents, out_key_weight, out_value_weight,
    *refs,
):
    count = len(PIECE)
    pieces = [Refs(PIECE, refs[h * count:(h + 1) * count]) for h in range(2)]
    s = Refs(SHARED, refs[2 * count:])
    me = Place()
    loads = [
        pltpu.make_async_copy(src, dst, s.load_sem.at[n])
        for n, (src, dst) in enumerate(
            ((latents, s.latents), (key_weight, s.key_weight), (value_weight, s.value_weight)))
    ]
    for load in loads:
        load.start()
    greet(
        [me.at_y(1), me.at_y(-1), me.at_z(1), me.at_z(-1)]
        + [me.at_head(d) for d in range(1, 2 * NX)]
        + [me.at_x(d) for d in range(1, NX)]
        + [me.at_low(d) for d in range(1, NL)]
    )
    for load in loads:
        load.wait()

    gain_k = key_gain[...]
    flat = s.latents[...]
    s.raw[...] = jnp.dot(flat, s.key_weight[...], preferred_element_type=F32)
    own_values = jnp.dot(flat, s.value_weight[...], preferred_element_type=F32).astype(BF16)
    for h, p in enumerate(pieces):
        cols = slice(h * HD, (h + 1) * HD)
        part = s.raw[:, cols]
        inverse = lax.rsqrt(jnp.mean(part * part, axis=1, keepdims=True) + EPS)
        p.keys[me.y, me.z] = (part * inverse * gain_k).astype(BF16)
        p.values[me.z, me.y] = own_values[:, cols]

    firsts, seconds = zip(*[gather_rings(me, p) for p in pieces])

    def start(rings, step):
        for ring in rings:
            ring.start(step)

    def follow(rings, step):
        for ring in rings:
            ring.wait(step)
            if step < 3:
                ring.start(step + 1)

    start(firsts[0], 0)
    start(firsts[1], 0)
    swaps = [Swap(me, p, h, queries, out_grad) for h, p in enumerate(pieces)]

    entries = []
    for t in range(2):
        entries.append([])
        for e in range(LIST):
            image = tile_list[me.yh * 2 + t, e]
            held = jnp.maximum(image, 0)
            slot = media_slot[held]
            entries[t].append((
                slot,
                jnp.where(image >= 0, media_position[held], DEAD),
                jnp.where(image >= 0, slot, SLOTS),
            ))
    gate = jnp.tanh(jnp.full((1, HD), gate_alpha[0], F32))
    gain_q = query_gain[...]
    for t in range(2):
        for c in range(2):
            s.key_sums[t, c, LIST] = jnp.zeros((LAT, HD), F32)
            s.value_sums[t, c, LIST] = jnp.zeros((LAT, HD), F32)

    for step in range(4):
        follow(firsts[0], step)
        follow(firsts[1], step)
    start(seconds[0], 0)
    follow(seconds[0], 0)
    follow(seconds[0], 1)
    start(seconds[1], 0)
    follow(seconds[0], 2)
    follow(seconds[1], 0)
    follow(seconds[0], 3)
    follow(seconds[1], 1)

    units = [(t, c) for t in range(2) for c in range(2)]

    def run(h, n):
        t, c = units[n]
        attend(me, pieces[h], s, t, c, entries, gate, gain_q)

    swaps[0].wait()
    run(0, 0)
    run(0, 1)
    follow(seconds[1], 2)
    run(0, 2)
    run(0, 3)
    to_slots(pieces[0], s, entries)
    sums = [reduce_rings(me, p) for p in pieces]
    raw_grads, value_grads, low_copies, head_copies = {}, {}, [], []

    def tasks(h):
        p = pieces[h]
        key_y, value_z, key_z, value_y, weight_z = sums[h]

        def begin():
            key_y.start()
            value_z.start()

        def first(step):
            def act():
                key_y.step(step)
                value_z.step(step)
            return act

        def turn():
            p.key_mid[...] = key_y.total().astype(BF16)
            key_z.start()
            p.value_mid[...] = value_z.total().astype(BF16)
            value_y.start()

        def second(step):
            def act():
                key_z.step(step)
                value_y.step(step)
            return act

        def own_image():
            key_sum = key_z.total()
            value_sum = value_y.total()
            part = s.raw[:, h * HD:(h + 1) * HD]
            inverse = lax.rsqrt(jnp.mean(part * part, axis=1, keepdims=True) + EPS)
            up = key_sum * gain_k
            row_inner = jnp.mean(up * part, axis=1, keepdims=True)
            raw_grads[h] = (inverse * (up - part * (inverse * inverse * row_inner))).astype(BF16)
            value_grads[h] = value_sum.astype(BF16)
            both = jnp.concatenate([raw_grads[h], value_grads[h]], axis=1)
            share = dot(s.latents[...], both, 0, 0)
            for n in range(SLOTS):
                block = share[n * 40:(n + 1) * 40]
                block = jnp.concatenate([block, jnp.zeros((PAD - 40, 2 * HD), F32)], axis=0)
                p.weights[n % NZ, n // NZ] = block.astype(BF16)
            weight_z.start()
            if h == 1:
                latent_share()

        def third(step):
            def act():
                weight_z.step(step)
            return act

        def low():
            p.low_out[...] = weight_z.total().astype(BF16)
            for d in range(1, NL):
                copy = remote(
                    p.low_out.at[lax.rem(me.yl + d, NL)], p.low_in.at[d], p.low_send, p.low_recv, d, me.at_low(d))
                copy.start()
                low_copies.append(copy)

        def last():
            total = p.low_out[me.yl].astype(F32)
            for d in range(1, NL):
                ref = p.low_in.at[d]
                remote(ref, ref, p.low_send, p.low_recv, d, me.at_low(d)).wait_recv()
                total = total + ref[...].astype(F32)
            cols = slice(h * HD, (h + 1) * HD)
            out_key_weight[:, cols] = total[0:40, 0:HD]
            out_value_weight[:, cols] = total[0:40, HD:]

        return (
            [begin] + [first(step) for step in (1, 2, 3)] + [turn] + [second(step) for step in (1, 2, 3)]
            + [own_image] + [third(step) for step in (1, 2, 3)] + [low, last]
        )

    def latent_share():
        raw_grad = jnp.concatenate([raw_grads[0], raw_grads[1]], axis=1)
        value_grad = jnp.concatenate([value_grads[0], value_grads[1]], axis=1)
        s.wide[...] = dot(raw_grad, s.key_weight[...], 1, 1) + dot(value_grad, s.value_weight[...], 1, 1)
        s.spread[...] = jnp.zeros_like(s.spread)
        for d in range(2 * NX):
            for n in range(VD // HD):
                s.spread[d, 4 * n:4 * n + 4, :] = s.wide[4 * d:4 * d + 4, n * HD:(n + 1) * HD]
        s.shares[...] = s.spread[...].astype(BF16)
        for d in range(1, 2 * NX):
            copy = remote(
                s.shares.at[lax.rem(me.head + d, 2 * NX)], s.shares_in.at[d], s.head_send, s.head_recv, d,
                me.at_head(d))
            copy.start()
            head_copies.append(copy)

    left = [tasks(0), tasks(1)]

    def go(h):
        left[h].pop(0)()

    go(0)
    backs = [SwapBack(me, pieces[0], 0, out_queries)]
    follow(seconds[1], 3)
    swaps[1].wait()
    run(1, 0)
    run(1, 1)
    go(0)
    run(1, 2)
    run(1, 3)
    to_slots(pieces[1], s, entries)
    go(1)
    go(0)
    backs.append(SwapBack(me, pieces[1], 1, out_queries))
    while left[1]:
        go(1)
        if left[0]:
            go(0)

    total = s.shares[me.head].astype(F32)
    for d in range(1, 2 * NX):
        ref = s.shares_in.at[d]
        remote(ref, ref, s.head_send, s.head_recv, d, me.at_head(d)).wait_recv()
        total = total + ref[...].astype(F32)
    s.spread[0] = total
    for n in range(VD // HD):
        s.wide[0:4, n * HD:(n + 1) * HD] = s.spread[0, 4 * n:4 * n + 4, :]
    out_latents[...] = s.wide[0:4, :].astype(BF16)

    for swap in swaps + backs:
        swap.finish()
    for copy in head_copies + low_copies:
        copy.wait_send()
    for rings in firsts + seconds + tuple(sums):
        for ring in rings:
            ring.finish()


VMEM = pl.BlockSpec(memory_space=pltpu.VMEM)
SMEM = pl.BlockSpec(memory_space=pltpu.SMEM)
HBM = pl.BlockSpec(memory_space=pl.ANY)
LIMIT = 60 * 1024 * 1024


def struct(shape, dtype):
    return jax.ShapeDtypeStruct(shape, dtype)


def body(
    queries,
    out_grad,
    latents,
    key_weight,
    value_weight,
    query_gain,
    key_gain,
    gate_alpha,
    media_slot,
    media_position,
    tile_list,
):
    query_grad, latent_grad, key_weight_grad, value_weight_grad = pl.pallas_call(
        kernel,
        out_shape=(
            struct((OWN, 2 * NX * COLS), BF16),
            struct((4, VD), BF16),
            struct((VD // SLOTS, COLS), F32),
            struct((VD // SLOTS, COLS), F32),
        ),
        in_specs=[SMEM] * 4 + [HBM] * 5 + [VMEM] * 2,
        out_specs=(HBM, VMEM, VMEM, VMEM),
        scratch_shapes=list(PIECE.values()) * 2 + list(SHARED.values()),
        compiler_params=pltpu.CompilerParams(collective_id=0, has_side_effects=True, vmem_limit_bytes=LIMIT),
        name="backward",
    )(
        tile_list, media_slot, media_position, gate_alpha,
        queries, out_grad, latents.reshape(LAT, VD), key_weight, value_weight,
        query_gain.reshape(1, HD), key_gain.reshape(1, HD),
    )
    return (query_grad, latent_grad.reshape(1, 4, VD), key_weight_grad, value_weight_grad)


def solution(mesh):
    in_specs = (
        P(("seq", "head"), None),
        P(("seq", "head"), None),
        P("seq", None, None),
        P(None, "head"),
        P(None, "head"),
        P(),
        P(),
        P(),
        P(),
        P(),
        P("seq", None),
    )
    out_specs = (
        P(("seq", "head"), None),
        P("seq", "head", None),
        P("seq", "head"),
        P("seq", "head"),
    )
    return jax.shard_map(body, mesh=mesh, in_specs=in_specs, out_specs=out_specs, check_vma=False)
```

time: 981 us -> 134 us (0.14); the launches traced: 965 us -> 133 us
  waiting for transfers between devices: 787 us -> 0 us
  Pallas kernels: 0 us -> 127 us
  local copies, waits for them, and re-layouts: 66.5 us -> 4.32 us
  matrix products: 58.9 us -> 0 us
  starting transfers between devices: 29.8 us -> 0 us
  between operations: 15.4 us -> 1.31 us
    unnamed x7 -> x0, waiting for transfers between devices: 310 us -> none
    reduce_scatter x2 -> x0, waiting for transfers between devices: 309 us -> none  [the longest x1 157 us: body(): lax.psum_scatter(value_part.astype(jnp.bfloat16), 'seq', scatter_dimensio...]
    pallas_call x0 -> x1, Pallas kernels: none -> 127 us  [body(): pl.pallas_call(kernel, out_shape=(struct((OWN, 2 * NX * COLS), BF16), str...]
    all_gather x1 -> x0, waiting for transfers between devices: 102 us -> none  [body(): lax.all_gather(latents, 'seq', axis=0, tiled=True)]
    all_to_all x3 -> x0, waiting for transfers between devices: 64.9 us -> none  [the longest x1 28.3 us: body(): lax.all_to_all(out_grad, 'head', split_axis=1, concat_axis=0, tiled=True)]
    dot_general x30 -> x0, matrix products: 58.9 us -> none  [the longest x4 12.3 us: attend(): jnp.einsum('hqk,khd->qhd', grad_scores, key_tile, preferred_element_type=...]
    all_to_all x3 -> x0, starting transfers between devices: 29.6 us -> none  [the longest x1 9.95 us: body(): lax.all_to_all(grad_queries.reshape(token_rows, local_width), 'head', spl...]
    dynamic_slice x24 -> x0, local copies, waits for them, and re-layouts: 20.8 us -> none  [body(): grad_queries, grad_keys, grad_values = lax.map(attend, tile_inputs)]
  transfers between devices with their start and end apart: 8 -> 0, of which waited for: 8 -> 0; matrix products, arithmetic and copies ran while one was open for 2% -> 0% of each run, Pallas kernels for 0% -> 0%
where the time goes in v2:
time: 134 us; the launch traced here: 133 us
  Pallas kernels  127 us (95%)
  local copies, waits for them, and re-layouts  4.32 us (3%)
    pallas_call x1, Pallas kernels, body(): pl.pallas_call(kernel, out_shape=(struct((OWN, 2 * NX * COLS), BF16), str...  127 us
    unnamed x10, local copies, waits for them, and re-layouts  4.32 us

profile of v2, /device:TPU:56, one launch (start us, length us, event | category | flops | bytes accessed | tf_op | source)
XLA Modules:
  0.0 132.8 jit_solution(13172640797984045119)
XLA Ops:
  1.3 127.2 %backward.1 = (bf16[128,4096]{1,0:T(8,128)(2,1)}, bf16[4,1280]{1,0:T(4,128)(2,1)}, f32[40,256]{1,0:T(8,128)}, f32[40,256]{1,0:T(8,128)}) custom-call(s32[4,8]{1,0:T(4,128)} %tile_list.1, s32[32]{0:T(128)} %media_slot.1, s32[32]{0:T(128)} %media_position.1, f32[1]{0:T(128)S(6)} %copy.19.gate_alpha, bf16[128,4096]{1,0:T(8,128)(2,1)} %queries.1, ...), custom_call_target="tpu_custom_call" | custom-call | tf_op jit(solution)/shard_map/backward/pallas_call | solution.py:655
  128.4 0.0 copy-start.2
  128.5 0.0 copy-start.1
  128.5 2.3 %copy.20 = bf16[128,4096]{1,0:T(8,128)(2,1)} copy(bf16[128,4096]{1,0:T(8,128)(2,1)} %get-tuple-element.16) | data formatting | bytes 2097152
  130.8 0.0 copy-done.2
  130.8 0.6 copy.21
  131.4 0.0 copy-done.1
  131.4 0.0 copy-start
  131.4 0.6 copy.22
  132.0 0.2 copy-done
  132.2 0.6 copy.23
Async XLA Ops:
  128.4 2.3 %copy-start.2 = (bf16[4,1280]{1,0:T(4,128)(2,1)S(1)}, bf16[4,1280]{1,0:T(4,128)(2,1)}, u32[]{:S(2)}) copy-start(bf16[4,1280]{1,0:T(4,128)(2,1)} %get-tuple-element.9) | copy-start | bytes 30724
  128.5 2.9 %copy-start.1 = (f32[40,256]{1,0:T(8,128)S(1)}, f32[40,256]{1,0:T(8,128)}, u32[]{:S(2)}) copy-start(f32[40,256]{1,0:T(8,128)} %get-tuple-element.18) | copy-start | bytes 122884
  131.4 0.8 copy-start

commit v3 on v2

--- a/solution.py
+++ b/solution.py
@@ -106,6 +106,30 @@
             copy.wait_send()
 
 
+class Direct:
+    def __init__(self, source, target, arrived, me, at, sends, recvs, base):
+        self.source, self.target, self.arrived, self.me, self.at = source, target, arrived, me, at
+        self.sends, self.recvs, self.base = sends, recvs, base
+        self.started = []
+
+    def start(self):
+        for d in (4, 3, 5, 2, 6, 1, 7):
+            index = lax.rem(self.me + d, 8)
+            copy = remote(
+                self.source(index), self.target(index, d), self.sends, self.recvs, self.base + d, self.at(d))
+            copy.start()
+            self.started.append(copy)
+
+    def wait(self, d):
+        ref = self.arrived(lax.rem(self.me + (8 - d), 8), d)
+        remote(ref, ref, self.sends, self.recvs, self.base + d, self.at(d)).wait_recv()
+        return ref
+
+    def finish(self):
+        for copy in self.started:
+            copy.wait_send()
+
+
 class ReduceRing:
     def __init__(self, own, inbox, me, right, left, sends, recvs, base):
         self.own, self.inbox, self.me, self.targets = own, inbox, me, (right, left)
@@ -178,14 +202,14 @@
     value_in=scratch(2, 4, NY, LAT, HD),
     key_mid=scratch(NZ, LAT, HD),
     value_mid=scratch(NY, LAT, HD),
-    key_low=scratch(2, 4, LAT, HD),
-    value_low=scratch(2, 4, LAT, HD),
-    weights=scratch(NZ, NL, PAD, 2 * HD),
-    weights_in=scratch(2, 4, NL, PAD, 2 * HD),
+    key_low=scratch(NZ, LAT, HD),
+    value_low=scratch(NY, LAT, HD),
+    weights=scratch(2, NZ, NL, PAD, HD),
+    weights_in=scratch(2, 2, 4, NL, PAD, HD),
     low_out=scratch(NL, PAD, 2 * HD),
     low_in=scratch(NL, PAD, 2 * HD),
-    ring_send=pltpu.SemaphoreType.DMA((72,)),
-    ring_recv=pltpu.SemaphoreType.DMA((72,)),
+    ring_send=pltpu.SemaphoreType.DMA((80,)),
+    ring_recv=pltpu.SemaphoreType.DMA((80,)),
     swap_send=pltpu.SemaphoreType.DMA((28,)),
     swap_recv=pltpu.SemaphoreType.DMA((28,)),
     swap_own=pltpu.SemaphoreType.DMA((4,)),
@@ -231,8 +255,12 @@
     y, z = (me.at_y(1), me.at_y(-1)), (me.at_z(1), me.at_z(-1))
     sems = (p.ring_send, p.ring_recv)
     first = (
-        GatherRing(lambda b, half: halves(p.keys.at[me.y, b], LAT // 2, half), me.z, *z, *sems, 0),
-        GatherRing(lambda b, half: halves(p.values.at[me.z, b], LAT // 2, half), me.y, *y, *sems, 8),
+        Direct(
+            lambda b: p.keys.at[me.y, me.z], lambda b, d: p.keys.at[me.y, me.z], lambda b, d: p.keys.at[me.y, b],
+            me.z, me.at_z, *sems, 0),
+        Direct(
+            lambda b: p.values.at[me.z, me.y], lambda b, d: p.values.at[me.z, me.y],
+            lambda b, d: p.values.at[me.z, b], me.y, me.at_y, *sems, 8),
     )
     second = (
         GatherRing(lambda b, half: halves(p.keys.at[b], NZ // 2, half), me.y, *y, *sems, 16),
@@ -248,13 +276,18 @@
         lambda b, half: halves(p.grad_keys.at[b], NZ // 2, half), inbox(p.key_in, NZ // 2), me.y, *y, *sems, 32)
     value_z = ReduceRing(
         lambda b, half: halves(p.grad_values.at[b], NY // 2, half), inbox(p.value_in, NY // 2), me.z, *z, *sems, 40)
-    key_z = ReduceRing(
-        lambda b, half: halves(p.key_mid.at[b], LAT // 2, half), inbox(p.key_low, LAT // 2), me.z, *z, *sems, 48)
-    value_y = ReduceRing(
-        lambda b, half: halves(p.value_mid.at[b], LAT // 2, half), inbox(p.value_low, LAT // 2), me.y, *y, *sems, 56)
-    weight_z = ReduceRing(
-        lambda b, half: halves(p.weights.at[b], NL // 2, half), inbox(p.weights_in, NL // 2), me.z, *z, *sems, 64)
-    return key_y, value_z, key_z, value_y, weight_z
+    key_z = Direct(
+        lambda b: p.key_mid.at[b], lambda b, d: p.key_low.at[d], lambda b, d: p.key_low.at[d], me.z, me.at_z, *sems, 48)
+    value_y = Direct(
+        lambda b: p.value_mid.at[b], lambda b, d: p.value_low.at[d], lambda b, d: p.value_low.at[d],
+        me.y, me.at_y, *sems, 56)
+    weight_z = [
+        ReduceRing(
+            lambda b, half, k=k: halves(p.weights.at[k, b], NL // 2, half), inbox(p.weights_in.at[k], NL // 2),
+            me.z, *z, *sems, 64 + 8 * k)
+        for k in range(2)
+    ]
+    return [key_y, value_z, key_z, value_y] + weight_z
 
 
 def columns(c, place, h):
@@ -416,10 +449,9 @@
     for load in loads:
         load.start()
     greet(
-        [me.at_y(1), me.at_y(-1), me.at_z(1), me.at_z(-1)]
+        [me.at_y(d) for d in range(1, NY)]
+        + [me.at_z(d) for d in range(1, NZ)]
         + [me.at_head(d) for d in range(1, 2 * NX)]
-        + [me.at_x(d) for d in range(1, NX)]
-        + [me.at_low(d) for d in range(1, NL)]
     )
     for load in loads:
         load.wait()
@@ -447,9 +479,10 @@
             if step < 3:
                 ring.start(step + 1)
 
-    start(firsts[0], 0)
-    start(firsts[1], 0)
-    swaps = [Swap(me, p, h, queries, out_grad) for h, p in enumerate(pieces)]
+    for rings in firsts:
+        for ring in rings:
+            ring.start()
+    swaps = [Swap(me, pieces[0], 0, queries, out_grad)]
 
     entries = []
     for t in range(2):
@@ -470,13 +503,16 @@
             s.key_sums[t, c, LIST] = jnp.zeros((LAT, HD), F32)
             s.value_sums[t, c, LIST] = jnp.zeros((LAT, HD), F32)
 
-    for step in range(4):
-        follow(firsts[0], step)
-        follow(firsts[1], step)
-    start(seconds[0], 0)
+    for rings, later in zip(firsts, seconds):
+        for ring in rings:
+            for d in range(1, 8):
+                ring.wait(d)
+        if rings is firsts[0]:
+            start(later, 0)
     follow(seconds[0], 0)
     follow(seconds[0], 1)
     start(seconds[1], 0)
+    swaps.append(Swap(me, pieces[1], 1, queries, out_grad))
     follow(seconds[0], 2)
     follow(seconds[1], 0)
     follow(seconds[0], 3)
@@ -500,7 +536,7 @@
 
     def tasks(h):
         p = pieces[h]
-        key_y, value_z, key_z, value_y, weight_z = sums[h]
+        key_y, value_z, key_z, value_y, *weight_z = sums[h]
 
         def begin():
             key_y.start()
@@ -518,38 +554,38 @@
             p.value_mid[...] = value_z.total().astype(BF16)
             value_y.start()
 
-        def second(step):
-            def act():
-                key_z.step(step)
-                value_y.step(step)
-            return act
-
         def own_image():
-            key_sum = key_z.total()
-            value_sum = value_y.total()
+            key_sum = p.key_mid[me.z].astype(F32)
+            for d in (1, 7, 2, 6, 3, 5, 4):
+                key_sum = key_sum + key_z.wait(d)[...].astype(F32)
+            value_sum = p.value_mid[me.y].astype(F32)
+            for d in (1, 7, 2, 6, 3, 5, 4):
+                value_sum = value_sum + value_y.wait(d)[...].astype(F32)
             part = s.raw[:, h * HD:(h + 1) * HD]
             inverse = lax.rsqrt(jnp.mean(part * part, axis=1, keepdims=True) + EPS)
             up = key_sum * gain_k
             row_inner = jnp.mean(up * part, axis=1, keepdims=True)
             raw_grads[h] = (inverse * (up - part * (inverse * inverse * row_inner))).astype(BF16)
             value_grads[h] = value_sum.astype(BF16)
-            both = jnp.concatenate([raw_grads[h], value_grads[h]], axis=1)
-            share = dot(s.latents[...], both, 0, 0)
-            for n in range(SLOTS):
-                block = share[n * 40:(n + 1) * 40]
-                block = jnp.concatenate([block, jnp.zeros((PAD - 40, 2 * HD), F32)], axis=0)
-                p.weights[n % NZ, n // NZ] = block.astype(BF16)
-            weight_z.start()
+            for k, grad in enumerate((raw_grads[h], value_grads[h])):
+                share = dot(s.latents[...], grad, 0, 0)
+                for n in range(SLOTS):
+                    block = share[n * 40:(n + 1) * 40]
+                    block = jnp.concatenate([block, jnp.zeros((PAD - 40, HD), F32)], axis=0)
+                    p.weights[k, n % NZ, n // NZ] = block.astype(BF16)
+                weight_z[k].start()
             if h == 1:
                 latent_share()
 
         def third(step):
             def act():
-                weight_z.step(step)
+                for ring in weight_z:
+                    ring.step(step)
             return act
 
         def low():
-            p.low_out[...] = weight_z.total().astype(BF16)
+            for k, ring in enumerate(weight_z):
+                p.low_out[:, :, k * HD:(k + 1) * HD] = ring.total().astype(BF16)
             for d in range(1, NL):
                 copy = remote(
                     p.low_out.at[lax.rem(me.yl + d, NL)], p.low_in.at[d], p.low_send, p.low_recv, d, me.at_low(d))
@@ -567,8 +603,8 @@
             out_value_weight[:, cols] = total[0:40, HD:]
 
         return (
-            [begin] + [first(step) for step in (1, 2, 3)] + [turn] + [second(step) for step in (1, 2, 3)]
-            + [own_image] + [third(step) for step in (1, 2, 3)] + [low, last]
+            [begin] + [first(step) for step in (1, 2, 3)] + [turn, own_image]
+            + [third(step) for step in (1, 2, 3)] + [low, last]
         )
 
     def latent_share():

time: 134 us -> 122 us (0.910)
  Pallas kernels: 127 us -> 116 us
    pallas_call x1, Pallas kernels: 127 us -> 116 us  [body(): pl.pallas_call(kernel, out_shape=(struct((OWN, 2 * NX * COLS), BF16), str...]
where the time goes in v3:
time: 122 us
  Pallas kernels  116 us (95%)
  local copies, waits for them, and re-layouts  4.32 us (4%)
  between operations  1.31 us (1%)
    pallas_call x1, Pallas kernels, body(): pl.pallas_call(kernel, out_shape=(struct((OWN, 2 * NX * COLS), BF16), str...  116 us
    unnamed x10, local copies, waits for them, and re-layouts  4.32 us

profile of v3, /device:TPU:56, one launch (start us, length us, event | category | flops | bytes accessed | tf_op | source)
XLA Modules:
  0.0 121.7 jit_solution(8421014681992968187)
XLA Ops:
  1.3 116.1 %backward.1 = (bf16[128,4096]{1,0:T(8,128)(2,1)}, bf16[4,1280]{1,0:T(4,128)(2,1)}, f32[40,256]{1,0:T(8,128)}, f32[40,256]{1,0:T(8,128)}) custom-call(s32[4,8]{1,0:T(4,128)} %tile_list.1, s32[32]{0:T(128)} %media_slot.1, s32[32]{0:T(128)} %media_position.1, f32[1]{0:T(128)S(6)} %copy.19.gate_alpha, bf16[128,4096]{1,0:T(8,128)(2,1)} %queries.1, ...), custom_call_target="tpu_custom_call" | custom-call | tf_op jit(solution)/shard_map/backward/pallas_call | solution.py:691
  117.3 0.0 copy-start.2
  117.4 0.0 copy-start.1
  117.4 2.3 %copy.20 = bf16[128,4096]{1,0:T(8,128)(2,1)} copy(bf16[128,4096]{1,0:T(8,128)(2,1)} %get-tuple-element.16) | data formatting | bytes 2097152
  119.7 0.0 copy-done.2
  119.7 0.6 copy.21
  120.3 0.0 copy-done.1
  120.3 0.0 copy-start
  120.3 0.6 copy.22
  120.9 0.2 copy-done
  121.1 0.6 copy.23
Async XLA Ops:
  117.3 2.3 %copy-start.2 = (bf16[4,1280]{1,0:T(4,128)(2,1)S(1)}, bf16[4,1280]{1,0:T(4,128)(2,1)}, u32[]{:S(2)}) copy-start(bf16[4,1280]{1,0:T(4,128)(2,1)} %get-tuple-element.9) | copy-start | bytes 30724
  117.4 2.9 %copy-start.1 = (f32[40,256]{1,0:T(8,128)S(1)}, f32[40,256]{1,0:T(8,128)}, u32[]{:S(2)}) copy-start(f32[40,256]{1,0:T(8,128)} %get-tuple-element.18) | copy-start | bytes 122884
  120.3 0.8 copy-start

commit v4 on v3

--- a/solution.py
+++ b/solution.py
@@ -63,10 +63,9 @@
 
 
 def greet(partners):
-    barrier = pltpu.get_barrier_semaphore()
     for partner in partners:
-        pl.semaphore_signal(barrier, inc=1, device_id=partner, device_id_type=MESH)
-    pl.semaphore_wait(barrier, len(partners))
+        pl.semaphore_signal(pltpu.get_barrier_semaphore(), inc=1, device_id=partner, device_id_type=MESH)
+    return lambda: pl.semaphore_wait(pltpu.get_barrier_semaphore(), len(partners))
 
 
 def remote(src, dst, sends, recvs, sem, device):
@@ -186,6 +185,10 @@
     return ref if half is None else ref.at[pl.ds(half * size, size)]
 
 
+def quarters(ref, part, half):
+    return ref.at[pl.ds(part * 4, 4)] if half is None else ref.at[pl.ds(part * 4 + half * 2, 2)]
+
+
 def scratch(*shape, dtype=BF16):
     return pltpu.VMEM(shape, dtype)
 
@@ -198,8 +201,8 @@
     grad_q=scratch(2, TOK, HD),
     grad_keys=scratch(NY, NZ, LAT, HD),
     grad_values=scratch(NZ, NY, LAT, HD),
-    key_in=scratch(2, 4, NZ, LAT, HD),
-    value_in=scratch(2, 4, NY, LAT, HD),
+    key_in=scratch(2, 2, 4, 4, LAT, HD),
+    value_in=scratch(2, 2, 4, 4, LAT, HD),
     key_mid=scratch(NZ, LAT, HD),
     value_mid=scratch(NY, LAT, HD),
     key_low=scratch(NZ, LAT, HD),
@@ -208,8 +211,8 @@
     weights_in=scratch(2, 2, 4, NL, PAD, HD),
     low_out=scratch(NL, PAD, 2 * HD),
     low_in=scratch(NL, PAD, 2 * HD),
-    ring_send=pltpu.SemaphoreType.DMA((80,)),
-    ring_recv=pltpu.SemaphoreType.DMA((80,)),
+    ring_send=pltpu.SemaphoreType.DMA((112,)),
+    ring_recv=pltpu.SemaphoreType.DMA((112,)),
     swap_send=pltpu.SemaphoreType.DMA((28,)),
     swap_recv=pltpu.SemaphoreType.DMA((28,)),
     swap_own=pltpu.SemaphoreType.DMA((4,)),
@@ -232,6 +235,8 @@
     shares_in=scratch(2 * NX, PAD, HD),
     spread=scratch(2 * NX, PAD, HD, dtype=F32),
     wide=scratch(LAT, VD, dtype=F32),
+    latents_t=scratch(VD, LAT),
+    places=pltpu.SMEM((2, SLOTS), jnp.int32),
     load_sem=pltpu.SemaphoreType.DMA((3,)),
     head_send=pltpu.SemaphoreType.DMA((16,)),
     head_recv=pltpu.SemaphoreType.DMA((16,)),
@@ -262,32 +267,42 @@
             lambda b: p.values.at[me.z, me.y], lambda b, d: p.values.at[me.z, me.y],
             lambda b, d: p.values.at[me.z, b], me.y, me.at_y, *sems, 8),
     )
-    second = (
-        GatherRing(lambda b, half: halves(p.keys.at[b], NZ // 2, half), me.y, *y, *sems, 16),
-        GatherRing(lambda b, half: halves(p.values.at[b], NY // 2, half), me.z, *z, *sems, 24),
-    )
+    second = []
+    for n in range(2):
+        second += [
+            GatherRing(lambda b, half, n=n: quarters(p.keys.at[b], n, half), me.y, *y, *sems, 16 + 8 * n),
+            GatherRing(lambda b, half, n=n: quarters(p.values.at[b], n, half), me.z, *z, *sems, 32 + 8 * n),
+        ]
     return first, second
 
 
 def reduce_rings(me, p):
     y, z = (me.at_y(1), me.at_y(-1)), (me.at_z(1), me.at_z(-1))
     sems = (p.ring_send, p.ring_recv)
-    key_y = ReduceRing(
-        lambda b, half: halves(p.grad_keys.at[b], NZ // 2, half), inbox(p.key_in, NZ // 2), me.y, *y, *sems, 32)
-    value_z = ReduceRing(
-        lambda b, half: halves(p.grad_values.at[b], NY // 2, half), inbox(p.value_in, NY // 2), me.z, *z, *sems, 40)
+    key_y = [
+        ReduceRing(
+            lambda b, half, n=n: quarters(p.grad_keys.at[b], n, half), inbox(p.key_in.at[n], 2),
+            me.y, *y, *sems, 48 + 8 * n)
+        for n in range(2)
+    ]
+    value_z = [
+        ReduceRing(
+            lambda b, half, n=n: quarters(p.grad_values.at[b], n, half), inbox(p.value_in.at[n], 2),
+            me.z, *z, *sems, 64 + 8 * n)
+        for n in range(2)
+    ]
     key_z = Direct(
-        lambda b: p.key_mid.at[b], lambda b, d: p.key_low.at[d], lambda b, d: p.key_low.at[d], me.z, me.at_z, *sems, 48)
+        lambda b: p.key_mid.at[b], lambda b, d: p.key_low.at[d], lambda b, d: p.key_low.at[d], me.z, me.at_z, *sems, 80)
     value_y = Direct(
         lambda b: p.value_mid.at[b], lambda b, d: p.value_low.at[d], lambda b, d: p.value_low.at[d],
-        me.y, me.at_y, *sems, 56)
+        me.y, me.at_y, *sems, 88)
     weight_z = [
         ReduceRing(
             lambda b, half, k=k: halves(p.weights.at[k, b], NL // 2, half), inbox(p.weights_in.at[k], NL // 2),
-            me.z, *z, *sems, 64 + 8 * k)
+            me.z, *z, *sems, 96 + 8 * k)
         for k in range(2)
     ]
-    return [key_y, value_z, key_z, value_y] + weight_z
+    return key_y, value_z, key_z, value_y, weight_z
 
 
 def columns(c, place, h):
@@ -411,21 +426,23 @@
     p.grad_q[c, base:base + TILE, :] = (inverse * (up - q * (inverse * inverse * row_inner))).astype(BF16)
 
 
-def to_slots(p, s, entries):
+def find_places(places, entries):
     def one_slot(slot, carry):
-        z = lax.rem(slot, NZ)
-        low = lax.div(slot, NZ)
-        place = []
         for t in range(2):
             found = jnp.int32(LIST)
             for e in range(LIST):
                 found = jnp.where(entries[t][e][2] == slot, e, found)
-            place.append(found)
+            places[t, slot] = found
+        return carry
+
+    lax.fori_loop(0, SLOTS, one_slot, 0)
+
+
+def to_slots(tile_sums, places, target):
+    def one_slot(slot, carry):
         for c in range(2):
-            p.grad_keys[c * NL + low, z] = (
-                s.key_sums[0, c, place[0]] + s.key_sums[1, c, place[1]]).astype(BF16)
-            p.grad_values[z, c * NL + low] = (
-                s.value_sums[0, c, place[0]] + s.value_sums[1, c, place[1]]).astype(BF16)
+            target(c, lax.div(slot, NZ), lax.rem(slot, NZ))[...] = (
+                tile_sums[0, c, places[0, slot]] + tile_sums[1, c, places[1, slot]]).astype(BF16)
         return carry
 
     lax.fori_loop(0, SLOTS, one_slot, 0)
@@ -448,7 +465,7 @@
     ]
     for load in loads:
         load.start()
-    greet(
+    wait_for_all = greet(
         [me.at_y(d) for d in range(1, NY)]
         + [me.at_z(d) for d in range(1, NZ)]
         + [me.at_head(d) for d in range(1, 2 * NX)]
@@ -466,6 +483,8 @@
         inverse = lax.rsqrt(jnp.mean(part * part, axis=1, keepdims=True) + EPS)
         p.keys[me.y, me.z] = (part * inverse * gain_k).astype(BF16)
         p.values[me.z, me.y] = own_values[:, cols]
+
+    wait_for_all()
 
     firsts, seconds = zip(*[gather_rings(me, p) for p in pieces])
 
@@ -503,6 +522,9 @@
             s.key_sums[t, c, LIST] = jnp.zeros((LAT, HD), F32)
             s.value_sums[t, c, LIST] = jnp.zeros((LAT, HD), F32)
 
+    find_places(s.places, entries)
+    s.latents_t[...] = flat.astype(F32).T.astype(BF16)
+
     for rings, later in zip(firsts, seconds):
         for ring in rings:
             for d in range(1, 8):
@@ -510,13 +532,11 @@
         if rings is firsts[0]:
             start(later, 0)
     follow(seconds[0], 0)
+    swaps.append(Swap(me, pieces[1], 1, queries, out_grad))
     follow(seconds[0], 1)
+    follow(seconds[0], 2)
     start(seconds[1], 0)
-    swaps.append(Swap(me, pieces[1], 1, queries, out_grad))
-    follow(seconds[0], 2)
-    follow(seconds[1], 0)
     follow(seconds[0], 3)
-    follow(seconds[1], 1)
 
     units = [(t, c) for t in range(2) for c in range(2)]
 
@@ -525,33 +545,38 @@
         attend(me, pieces[h], s, t, c, entries, gate, gain_q)
 
     swaps[0].wait()
-    run(0, 0)
-    run(0, 1)
-    follow(seconds[1], 2)
-    run(0, 2)
-    run(0, 3)
-    to_slots(pieces[0], s, entries)
+    for n in range(4):
+        run(0, n)
+        if n < 3:
+            follow(seconds[1], n)
     sums = [reduce_rings(me, p) for p in pieces]
     raw_grads, value_grads, low_copies, head_copies = {}, {}, [], []
 
     def tasks(h):
         p = pieces[h]
-        key_y, value_z, key_z, value_y, *weight_z = sums[h]
+        key_y, value_z, key_z, value_y, weight_z = sums[h]
 
         def begin():
-            key_y.start()
-            value_z.start()
+            to_slots(s.key_sums, s.places, lambda c, low, z: p.grad_keys.at[c * NL + low, z])
+            for ring in key_y:
+                ring.start()
+            to_slots(s.value_sums, s.places, lambda c, low, z: p.grad_values.at[z, c * NL + low])
+            for ring in value_z:
+                ring.start()
 
         def first(step):
             def act():
-                key_y.step(step)
-                value_z.step(step)
+                for pair in zip(key_y, value_z):
+                    for ring in pair:
+                        ring.step(step)
             return act
 
         def turn():
-            p.key_mid[...] = key_y.total().astype(BF16)
+            for n, ring in enumerate(key_y):
+                p.key_mid[n * 4:n * 4 + 4] = ring.total().astype(BF16)
             key_z.start()
-            p.value_mid[...] = value_z.total().astype(BF16)
+            for n, ring in enumerate(value_z):
+                p.value_mid[n * 4:n * 4 + 4] = ring.total().astype(BF16)
             value_y.start()
 
         def own_image():
@@ -567,20 +592,21 @@
             row_inner = jnp.mean(up * part, axis=1, keepdims=True)
             raw_grads[h] = (inverse * (up - part * (inverse * inverse * row_inner))).astype(BF16)
             value_grads[h] = value_sum.astype(BF16)
-            for k, grad in enumerate((raw_grads[h], value_grads[h])):
-                share = dot(s.latents[...], grad, 0, 0)
+            both = jnp.concatenate([raw_grads[h], value_grads[h]], axis=1)
+            share = jnp.dot(s.latents_t[...], both, preferred_element_type=F32)
+            for k in range(2):
                 for n in range(SLOTS):
-                    block = share[n * 40:(n + 1) * 40]
+                    block = share[n * 40:(n + 1) * 40, k * HD:(k + 1) * HD]
                     block = jnp.concatenate([block, jnp.zeros((PAD - 40, HD), F32)], axis=0)
                     p.weights[k, n % NZ, n // NZ] = block.astype(BF16)
                 weight_z[k].start()
-            if h == 1:
-                latent_share()
 
         def third(step):
             def act():
                 for ring in weight_z:
                     ring.step(step)
+                if h == 1 and step == 1:
+                    latent_share()
             return act
 
         def low():
@@ -637,7 +663,6 @@
     go(0)
     run(1, 2)
     run(1, 3)
-    to_slots(pieces[1], s, entries)
     go(1)
     go(0)
     backs.append(SwapBack(me, pieces[1], 1, out_queries))
@@ -660,9 +685,23 @@
         swap.finish()
     for copy in head_copies + low_copies:
         copy.wait_send()
-    for rings in firsts + seconds + tuple(sums):
+    for rings in firsts + seconds:
         for ring in rings:
             ring.finish()
+    for key_y, value_z, key_z, value_y, weight_z in sums:
+        for ring in key_y + value_z + [key_z, value_y] + weight_z:
+            ring.finish()
+
+
+def hand_on(*refs):
+    sources, results, sems = refs[:4], refs[4:8], refs[8]
+    copies = [
+        pltpu.make_async_copy(src, dst, sems.at[n]) for n, (src, dst) in enumerate(zip(sources, results))
+    ]
+    for copy in copies:
+        copy.start()
+    for copy in copies:
+        copy.wait()
 
 
 VMEM = pl.BlockSpec(memory_space=pltpu.VMEM)
@@ -688,14 +727,15 @@
     media_position,
     tile_list,
 ):
-    query_grad, latent_grad, key_weight_grad, value_weight_grad = pl.pallas_call(
+    shapes = (
+        struct((OWN, 2 * NX * COLS), BF16),
+        struct((4, VD), BF16),
+        struct((VD // SLOTS, COLS), F32),
+        struct((VD // SLOTS, COLS), F32),
+    )
+    grads = pl.pallas_call(
         kernel,
-        out_shape=(
-            struct((OWN, 2 * NX * COLS), BF16),
-            struct((4, VD), BF16),
-            struct((VD // SLOTS, COLS), F32),
-            struct((VD // SLOTS, COLS), F32),
-        ),
+        out_shape=shapes,
         in_specs=[SMEM] * 4 + [HBM] * 5 + [VMEM] * 2,
         out_specs=(HBM, VMEM, VMEM, VMEM),
         scratch_shapes=list(PIECE.values()) * 2 + list(SHARED.values()),
@@ -706,6 +746,15 @@
         queries, out_grad, latents.reshape(LAT, VD), key_weight, value_weight,
         query_gain.reshape(1, HD), key_gain.reshape(1, HD),
     )
+    query_grad, latent_grad, key_weight_grad, value_weight_grad = pl.pallas_call(
+        hand_on,
+        out_shape=shapes,
+        in_specs=[HBM] * 4,
+        out_specs=(HBM,) * 4,
+        scratch_shapes=[pltpu.SemaphoreType.DMA((4,))],
+        compiler_params=pltpu.CompilerParams(vmem_limit_bytes=LIMIT),
+        name="hand_on",
+    )(*grads)
     return (query_grad, latent_grad.reshape(1, 4, VD), key_weight_grad, value_weight_grad)
 
 

time: 122 us -> 150 us (1.23)
  Pallas kernels: 116 us -> 148 us
  local copies, waits for them, and re-layouts: 4.32 us -> 0 us
    pallas_call x1 -> x2, Pallas kernels: 116 us -> 148 us  [the longest x1 112 us: body(): pl.pallas_call(kernel, out_shape=shapes, in_specs=[SMEM] * 4 + [HBM] * 5...]
    unnamed x10 -> x0, local copies, waits for them, and re-layouts: 4.32 us -> none
where the time goes in v4:
time: 150 us; the launch traced here: 149 us
  Pallas kernels  148 us (99%)
    pallas_call x1, Pallas kernels, body(): pl.pallas_call(kernel, out_shape=shapes, in_specs=[SMEM] * 4 + [HBM] * 5...  112 us
    pallas_call x1, Pallas kernels, body(): pl.pallas_call(hand_on, out_shape=shapes, in_specs=[HBM] * 4, out_specs=(...  35.7 us

profile of v4, /device:TPU:56, one launch (start us, length us, event | category | flops | bytes accessed | tf_op | source)
XLA Modules:
  0.0 149.0 jit_solution(1075285508963738738)
XLA Ops:
  1.3 111.9 %backward.1 = (bf16[128,4096]{1,0:T(8,128)(2,1)}, bf16[4,1280]{1,0:T(4,128)(2,1)}, f32[40,256]{1,0:T(8,128)}, f32[40,256]{1,0:T(8,128)}) custom-call(s32[4,8]{1,0:T(4,128)} %tile_list.1, s32[32]{0:T(128)} %media_slot.1, s32[32]{0:T(128)} %media_position.1, f32[1]{0:T(128)S(6)} %copy.15.gate_alpha, bf16[128,4096]{1,0:T(8,128)(2,1)} %queries.1, ...), custom_call_target="tpu_custom_call" | custom-call | tf_op jit(solution)/shard_map/backward/pallas_call | solution.py:736
  113.2 35.7 %hand_on.1 = (bf16[128,4096]{1,0:T(8,128)(2,1)}, bf16[4,1280]{1,0:T(4,128)(2,1)}, f32[40,256]{1,0:T(8,128)}, f32[40,256]{1,0:T(8,128)}) custom-call(bf16[128,4096]{1,0:T(8,128)(2,1)} %get-tuple-element.12.refs_0_, bf16[4,1280]{1,0:T(4,128)(2,1)} %get-tuple-element.13.refs_1_, f32[40,256]{1,0:T(8,128)} %get-tuple-element.14.refs_2_, ...), custom_call_target="tpu_custom_call" | custom-call | tf_op jit(solution)/shard_map/hand_on/pallas_call | solution.py:749

commit v5 on v4

--- a/solution.py
+++ b/solution.py
@@ -196,9 +196,6 @@
 PIECE = dict(
     keys=scratch(NY, NZ, LAT, HD),
     values=scratch(NZ, NY, LAT, HD),
-    q_rows=scratch(2, TOK, HD),
-    g_rows=scratch(2, TOK, HD),
-    grad_q=scratch(2, TOK, HD),
     grad_keys=scratch(NY, NZ, LAT, HD),
     grad_values=scratch(NZ, NY, LAT, HD),
     key_in=scratch(2, 2, 4, 4, LAT, HD),
@@ -213,16 +210,19 @@
     low_in=scratch(NL, PAD, 2 * HD),
     ring_send=pltpu.SemaphoreType.DMA((112,)),
     ring_recv=pltpu.SemaphoreType.DMA((112,)),
+    low_send=pltpu.SemaphoreType.DMA((4,)),
+    low_recv=pltpu.SemaphoreType.DMA((4,)),
+)
+SHARED = dict(
+    q_rows=scratch(2, TOK, COLS),
+    g_rows=scratch(2, TOK, COLS),
+    grad_q=scratch(2, TOK, COLS),
     swap_send=pltpu.SemaphoreType.DMA((28,)),
     swap_recv=pltpu.SemaphoreType.DMA((28,)),
     swap_own=pltpu.SemaphoreType.DMA((4,)),
     back_send=pltpu.SemaphoreType.DMA((14,)),
     back_recv=pltpu.SemaphoreType.DMA((14,)),
     back_own=pltpu.SemaphoreType.DMA((2,)),
-    low_send=pltpu.SemaphoreType.DMA((4,)),
-    low_recv=pltpu.SemaphoreType.DMA((4,)),
-)
-SHARED = dict(
     latents=scratch(LAT, VD),
     key_weight=scratch(VD, COLS),
     value_weight=scratch(VD, COLS),
@@ -305,8 +305,8 @@
     return key_y, value_z, key_z, value_y, weight_z
 
 
-def columns(c, place, h):
-    return pl.ds(pl.multiple_of((c * NX + place) * COLS + h * HD, HD), HD)
+def columns(c, place):
+    return pl.ds(pl.multiple_of((c * NX + place) * COLS, COLS), COLS)
 
 
 def rows_of(place):
@@ -314,14 +314,14 @@
 
 
 class Swap:
-    def __init__(self, me, p, h, queries, out_grad):
+    def __init__(self, me, p, queries, out_grad):
         self.me, self.p = me, p
         self.sent, self.own = [], []
-        for d in range(NX):
-            to = lax.rem(me.xc + d, NX)
-            for n, (src, dst) in enumerate(((queries, p.q_rows), (out_grad, p.g_rows))):
-                for c in range(2):
-                    src_ref = src.at[:, columns(c, to, h)]
+        for c in range(2):
+            for d in range(NX):
+                to = lax.rem(me.xc + d, NX)
+                for n, (src, dst) in enumerate(((queries, p.q_rows), (out_grad, p.g_rows))):
+                    src_ref = src.at[:, columns(c, to)]
                     dst_ref = dst.at[c, rows_of(me.xc)]
                     if d == 0:
                         copy = pltpu.make_async_copy(src_ref, dst_ref, p.swap_own.at[n * 2 + c])
@@ -332,16 +332,15 @@
                         self.sent.append(copy)
                     copy.start()
 
-    def wait(self):
+    def wait(self, c):
         me, p = self.me, self.p
         for d in range(1, NX):
             source = lax.rem(me.xc + (NX - d), NX)
             for n, dst in enumerate((p.q_rows, p.g_rows)):
-                for c in range(2):
-                    ref = dst.at[c, rows_of(source)]
-                    sem = (d - 1) * 4 + n * 2 + c
-                    remote(ref, ref, p.swap_send, p.swap_recv, sem, me.at_x(d)).wait_recv()
-        for copy in self.own:
+                ref = dst.at[c, rows_of(source)]
+                sem = (d - 1) * 4 + n * 2 + c
+                remote(ref, ref, p.swap_send, p.swap_recv, sem, me.at_x(d)).wait_recv()
+        for copy in self.own[c * 2:c * 2 + 2]:
             copy.wait()
 
     def finish(self):
@@ -350,14 +349,14 @@
 
 
 class SwapBack:
-    def __init__(self, me, p, h, out):
-        self.me, self.p, self.h, self.out = me, p, h, out
+    def __init__(self, me, p, out):
+        self.me, self.p, self.out = me, p, out
         self.sent, self.own = [], []
         for d in range(NX):
             to = lax.rem(me.xc + d, NX)
             for c in range(2):
                 src_ref = p.grad_q.at[c, rows_of(to)]
-                dst_ref = out.at[:, columns(c, me.xc, h)]
+                dst_ref = out.at[:, columns(c, me.xc)]
                 if d == 0:
                     copy = pltpu.make_async_copy(src_ref, dst_ref, p.back_own.at[c])
                     self.own.append(copy)
@@ -371,7 +370,7 @@
         for d in range(1, NX):
             source = lax.rem(me.xc + (NX - d), NX)
             for c in range(2):
-                ref = self.out.at[:, columns(c, source, self.h)]
+                ref = self.out.at[:, columns(c, source)]
                 remote(ref, ref, p.back_send, p.back_recv, (d - 1) * 2 + c, me.at_x(d)).wait_recv()
         for copy in self.own:
             copy.wait()
@@ -379,7 +378,7 @@
             copy.wait_send()
 
 
-def attend(me, p, s, t, c, entries, gate, gain):
+def attend(me, p, s, h, t, c, entries, gate, gain):
     for e in range(LIST):
         rows = slice(e * LAT, (e + 1) * LAT)
         slot = entries[t][e][0]
@@ -388,8 +387,9 @@
     kt = s.key_tile[...]
     vt = s.value_tile[...]
     base = t * TILE
-    q = p.q_rows[c, base:base + TILE, :].astype(F32)
-    g = p.g_rows[c, base:base + TILE, :].astype(F32)
+    cols = slice(h * HD, (h + 1) * HD)
+    q = s.q_rows[c, base:base + TILE, cols].astype(F32)
+    g = s.g_rows[c, base:base + TILE, cols].astype(F32)
     inverse = lax.rsqrt(jnp.mean(q * q, axis=1, keepdims=True) + EPS)
     q_hat = (q * inverse * gain).astype(BF16)
     ctx = (gate * g).astype(BF16)
@@ -423,7 +423,7 @@
     s.value_sums[t, c, 0:LIST] = dot(probs, ctx, 1, 0).reshape(LIST, LAT, HD)
     up = dot(kt.T, grads, 1, 0).T * SCALE * gain
     row_inner = jnp.mean(up * q, axis=1, keepdims=True)
-    p.grad_q[c, base:base + TILE, :] = (inverse * (up - q * (inverse * inverse * row_inner))).astype(BF16)
+    s.grad_q[c, base:base + TILE, cols] = (inverse * (up - q * (inverse * inverse * row_inner))).astype(BF16)
 
 
 def find_places(places, entries):
@@ -501,7 +501,7 @@
     for rings in firsts:
         for ring in rings:
             ring.start()
-    swaps = [Swap(me, pieces[0], 0, queries, out_grad)]
+    swap = Swap(me, s, queries, out_grad)
 
     entries = []
     for t in range(2):
@@ -529,26 +529,25 @@
         for ring in rings:
             for d in range(1, 8):
                 ring.wait(d)
-        if rings is firsts[0]:
-            start(later, 0)
-    follow(seconds[0], 0)
-    swaps.append(Swap(me, pieces[1], 1, queries, out_grad))
-    follow(seconds[0], 1)
-    follow(seconds[0], 2)
-    start(seconds[1], 0)
+        start(later, 0)
+    for step in range(3):
+        follow(seconds[0], step)
+        follow(seconds[1], step)
     follow(seconds[0], 3)
 
-    units = [(t, c) for t in range(2) for c in range(2)]
+    units = [(t, c) for c in range(2) for t in range(2)]
 
     def run(h, n):
         t, c = units[n]
-        attend(me, pieces[h], s, t, c, entries, gate, gain_q)
-
-    swaps[0].wait()
-    for n in range(4):
-        run(0, n)
-        if n < 3:
-            follow(seconds[1], n)
+        attend(me, pieces[h], s, h, t, c, entries, gate, gain_q)
+
+    swap.wait(0)
+    run(0, 0)
+    follow(seconds[1], 3)
+    run(0, 1)
+    swap.wait(1)
+    run(0, 2)
+    run(0, 3)
     sums = [reduce_rings(me, p) for p in pieces]
     raw_grads, value_grads, low_copies, head_copies = {}, {}, [], []
 
@@ -655,9 +654,6 @@
         left[h].pop(0)()
 
     go(0)
-    backs = [SwapBack(me, pieces[0], 0, out_queries)]
-    follow(seconds[1], 3)
-    swaps[1].wait()
     run(1, 0)
     run(1, 1)
     go(0)
@@ -665,7 +661,7 @@
     run(1, 3)
     go(1)
     go(0)
-    backs.append(SwapBack(me, pieces[1], 1, out_queries))
+    back = SwapBack(me, s, out_queries)
     while left[1]:
         go(1)
         if left[0]:
@@ -681,8 +677,8 @@
         s.wide[0:4, n * HD:(n + 1) * HD] = s.spread[0, 4 * n:4 * n + 4, :]
     out_latents[...] = s.wide[0:4, :].astype(BF16)
 
-    for swap in swaps + backs:
-        swap.finish()
+    back.finish()
+    swap.finish()
     for copy in head_copies + low_copies:
         copy.wait_send()
     for rings in firsts + seconds:
@@ -694,14 +690,8 @@
 
 
 def hand_on(*refs):
-    sources, results, sems = refs[:4], refs[4:8], refs[8]
-    copies = [
-        pltpu.make_async_copy(src, dst, sems.at[n]) for n, (src, dst) in enumerate(zip(sources, results))
-    ]
-    for copy in copies:
-        copy.start()
-    for copy in copies:
-        copy.wait()
+    for source, result in zip(refs[:4], refs[4:]):
+        result[...] = source[...]
 
 
 VMEM = pl.BlockSpec(memory_space=pltpu.VMEM)
@@ -749,9 +739,8 @@
     query_grad, latent_grad, key_weight_grad, value_weight_grad = pl.pallas_call(
         hand_on,
         out_shape=shapes,
-        in_specs=[HBM] * 4,
-        out_specs=(HBM,) * 4,
-        scratch_shapes=[pltpu.SemaphoreType.DMA((4,))],
+        in_specs=[VMEM] * 4,
+        out_specs=(VMEM,) * 4,
         compiler_params=pltpu.CompilerParams(vmem_limit_bytes=LIMIT),
         name="hand_on",
     )(*grads)

time: 150 us -> 114 us (0.76)
  Pallas kernels: 148 us -> 111 us
    pallas_call x1, Pallas kernels: 35.7 us -> 2.29 us  [body(): pl.pallas_call(hand_on, out_shape=shapes, in_specs=[VMEM] * 4, out_specs=...]
    pallas_call x1, Pallas kernels: 112 us -> 109 us  [body(): pl.pallas_call(kernel, out_shape=shapes, in_specs=[SMEM] * 4 + [HBM] * 5...]
where the time goes in v5:
time: 114 us; the launch traced here: 112 us
  Pallas kernels  111 us (97%)
  between operations  1.29 us (1%)
    pallas_call x1, Pallas kernels, body(): pl.pallas_call(kernel, out_shape=shapes, in_specs=[SMEM] * 4 + [HBM] * 5...  109 us
    pallas_call x1, Pallas kernels, body(): pl.pallas_call(hand_on, out_shape=shapes, in_specs=[VMEM] * 4, out_specs=...  2.29 us

profile of v5, /device:TPU:56, one launch (start us, length us, event | category | flops | bytes accessed | tf_op | source)
XLA Modules:
  0.0 112.4 jit_solution(3214435146275299970)
XLA Ops:
  1.3 108.8 %backward.1 = (bf16[128,4096]{1,0:T(8,128)(2,1)}, bf16[4,1280]{1,0:T(4,128)(2,1)}, f32[40,256]{1,0:T(8,128)}, f32[40,256]{1,0:T(8,128)}) custom-call(s32[4,8]{1,0:T(4,128)} %tile_list.1, s32[32]{0:T(128)} %media_slot.1, s32[32]{0:T(128)} %media_position.1, f32[1]{0:T(128)S(6)} %copy.15.gate_alpha, bf16[128,4096]{1,0:T(8,128)(2,1)} %queries.1, ...), custom_call_target="tpu_custom_call" | custom-call | tf_op jit(solution)/shard_map/backward/pallas_call | solution.py:726
  110.1 2.3 %hand_on.1 = (bf16[128,4096]{1,0:T(8,128)(2,1)}, bf16[4,1280]{1,0:T(4,128)(2,1)}, f32[40,256]{1,0:T(8,128)}, f32[40,256]{1,0:T(8,128)}) custom-call(bf16[128,4096]{1,0:T(8,128)(2,1)} %get-tuple-element.12.refs_0_, bf16[4,1280]{1,0:T(4,128)(2,1)} %get-tuple-element.13.refs_1_, f32[40,256]{1,0:T(8,128)} %get-tuple-element.14.refs_2_, ...), custom_call_target="tpu_custom_call" | custom-call | tf_op jit(solution)/shard_map/hand_on/pallas_call | solution.py:739

commit v6 on v5

--- a/solution.py
+++ b/solution.py
@@ -90,15 +90,17 @@
         ref = self.block(lax.rem(self.me + (offset + 8), 8), way if step == 3 else None)
         return remote(ref, ref, self.sends, self.recvs, self.base + way * 4 + step, self.targets[way])
 
-    def start(self, step):
-        for way in (0, 1):
+    def start(self, step, ways=(0, 1)):
+        for way in ways:
             copy = self.copy(way, step, 0)
             copy.start()
             self.started.append(copy)
 
-    def wait(self, step):
+    def follow(self, step):
         for way in (0, 1):
             self.copy(way, step, 1).wait_recv()
+            if step < 3:
+                self.start(step + 1, (way,))
 
     def finish(self):
         for copy in self.started:
@@ -204,10 +206,16 @@
     value_mid=scratch(NY, LAT, HD),
     key_low=scratch(NZ, LAT, HD),
     value_low=scratch(NY, LAT, HD),
-    weights=scratch(2, NZ, NL, PAD, HD),
-    weights_in=scratch(2, 2, 4, NL, PAD, HD),
-    low_out=scratch(NL, PAD, 2 * HD),
-    low_in=scratch(NL, PAD, 2 * HD),
+    weights=scratch(NZ, NL, PAD, HD),
+    weights_in=scratch(2, 4, NL, PAD, HD),
+    low_out=scratch(NL, PAD, HD),
+    low_in=scratch(NL, PAD, HD),
+    wide_out=scratch(NL, NZ, PAD, HD),
+    wide_in=scratch(NL, NZ, PAD, HD),
+    line_out=scratch(NZ, PAD, HD),
+    line_in=scratch(NZ, PAD, HD),
+    wide_send=pltpu.SemaphoreType.DMA((4,)),
+    wide_recv=pltpu.SemaphoreType.DMA((4,)),
     ring_send=pltpu.SemaphoreType.DMA((112,)),
     ring_recv=pltpu.SemaphoreType.DMA((112,)),
     low_send=pltpu.SemaphoreType.DMA((4,)),
@@ -296,13 +304,12 @@
     value_y = Direct(
         lambda b: p.value_mid.at[b], lambda b, d: p.value_low.at[d], lambda b, d: p.value_low.at[d],
         me.y, me.at_y, *sems, 88)
-    weight_z = [
-        ReduceRing(
-            lambda b, half, k=k: halves(p.weights.at[k, b], NL // 2, half), inbox(p.weights_in.at[k], NL // 2),
-            me.z, *z, *sems, 96 + 8 * k)
-        for k in range(2)
-    ]
-    return key_y, value_z, key_z, value_y, weight_z
+    weight_z = ReduceRing(
+        lambda b, half: halves(p.weights.at[b], NL // 2, half), inbox(p.weights_in, NL // 2), me.z, *z, *sems, 96)
+    line_z = Direct(
+        lambda b: p.line_out.at[b], lambda b, d: p.line_in.at[d], lambda b, d: p.line_in.at[d],
+        me.z, me.at_z, *sems, 104)
+    return key_y, value_z, key_z, value_y, weight_z, line_z
 
 
 def columns(c, place):
@@ -494,9 +501,7 @@
 
     def follow(rings, step):
         for ring in rings:
-            ring.wait(step)
-            if step < 3:
-                ring.start(step + 1)
+            ring.follow(step)
 
     for rings in firsts:
         for ring in rings:
@@ -553,7 +558,7 @@
 
     def tasks(h):
         p = pieces[h]
-        key_y, value_z, key_z, value_y, weight_z = sums[h]
+        key_y, value_z, key_z, value_y, weight_z, line_z = sums[h]
 
         def begin():
             to_slots(s.key_sums, s.places, lambda c, low, z: p.grad_keys.at[c * NL + low, z])
@@ -593,39 +598,54 @@
             value_grads[h] = value_sum.astype(BF16)
             both = jnp.concatenate([raw_grads[h], value_grads[h]], axis=1)
             share = jnp.dot(s.latents_t[...], both, preferred_element_type=F32)
-            for k in range(2):
+            for k in (1, 0):
                 for n in range(SLOTS):
                     block = share[n * 40:(n + 1) * 40, k * HD:(k + 1) * HD]
-                    block = jnp.concatenate([block, jnp.zeros((PAD - 40, HD), F32)], axis=0)
-                    p.weights[k, n % NZ, n // NZ] = block.astype(BF16)
-                weight_z[k].start()
+                    block = jnp.concatenate([block, jnp.zeros((PAD - 40, HD), F32)], axis=0).astype(BF16)
+                    if k == 0:
+                        p.weights[n % NZ, n // NZ] = block
+                    else:
+                        p.wide_out[n // NZ, n % NZ] = block
+                if k == 0:
+                    weight_z.start()
+                else:
+                    to_low(p.wide_out, p.wide_in, p.wide_send, p.wide_recv)
+
+        def to_low(out, place, sends, recvs):
+            for d in (2, 1, 3):
+                copy = remote(out.at[lax.rem(me.yl + d, NL)], place.at[d], sends, recvs, d, me.at_low(d))
+                copy.start()
+                low_copies.append(copy)
+
+        def from_low(out, place, sends, recvs):
+            total = out[me.yl].astype(F32)
+            for d in (1, 3, 2):
+                ref = place.at[d]
+                remote(ref, ref, sends, recvs, d, me.at_low(d)).wait_recv()
+                total = total + ref[...].astype(F32)
+            return total
 
         def third(step):
             def act():
-                for ring in weight_z:
-                    ring.step(step)
+                weight_z.step(step)
+                if step == 3:
+                    p.line_out[...] = from_low(p.wide_out, p.wide_in, p.wide_send, p.wide_recv).astype(BF16)
+                    line_z.start()
                 if h == 1 and step == 1:
                     latent_share()
             return act
 
         def low():
-            for k, ring in enumerate(weight_z):
-                p.low_out[:, :, k * HD:(k + 1) * HD] = ring.total().astype(BF16)
-            for d in range(1, NL):
-                copy = remote(
-                    p.low_out.at[lax.rem(me.yl + d, NL)], p.low_in.at[d], p.low_send, p.low_recv, d, me.at_low(d))
-                copy.start()
-                low_copies.append(copy)
+            p.low_out[...] = weight_z.total().astype(BF16)
+            to_low(p.low_out, p.low_in, p.low_send, p.low_recv)
 
         def last():
-            total = p.low_out[me.yl].astype(F32)
-            for d in range(1, NL):
-                ref = p.low_in.at[d]
-                remote(ref, ref, p.low_send, p.low_recv, d, me.at_low(d)).wait_recv()
-                total = total + ref[...].astype(F32)
             cols = slice(h * HD, (h + 1) * HD)
-            out_key_weight[:, cols] = total[0:40, 0:HD]
-            out_value_weight[:, cols] = total[0:40, HD:]
+            total = p.line_out[me.z].astype(F32)
+            for d in (1, 7, 2, 6, 3, 5, 4):
+                total = total + line_z.wait(d)[...].astype(F32)
+            out_value_weight[:, cols] = total[0:40]
+            out_key_weight[:, cols] = from_low(p.low_out, p.low_in, p.low_send, p.low_recv)[0:40]
 
         return (
             [begin] + [first(step) for step in (1, 2, 3)] + [turn, own_image]
@@ -684,8 +704,8 @@
     for rings in firsts + seconds:
         for ring in rings:
             ring.finish()
-    for key_y, value_z, key_z, value_y, weight_z in sums:
-        for ring in key_y + value_z + [key_z, value_y] + weight_z:
+    for key_y, value_z, key_z, value_y, weight_z, line_z in sums:
+        for ring in key_y + value_z + [key_z, value_y, weight_z, line_z]:
             ring.finish()
 
 

time: 114 us -> 124 us (1.088)
  the two profiles are of different devices: /device:TPU:56 before, /device:TPU:64 now
where the time goes in v6:
time: 124 us
  Pallas kernels  123 us (99%)
  between operations  1.29 us (1%)
    pallas_call x1, Pallas kernels, body(): pl.pallas_call(kernel, out_shape=shapes, in_specs=[SMEM] * 4 + [HBM] * 5...  120 us

profile of v6, /device:TPU:64, one launch (start us, length us, event | category | flops | bytes accessed | tf_op | source)
XLA Modules:
  0.0 124.0 jit_solution(14144202760839517477)
XLA Ops:
  1.3 120.4 %backward.1 = (bf16[128,4096]{1,0:T(8,128)(2,1)}, bf16[4,1280]{1,0:T(4,128)(2,1)}, f32[40,256]{1,0:T(8,128)}, f32[40,256]{1,0:T(8,128)}) custom-call(s32[4,8]{1,0:T(4,128)} %tile_list.1, s32[32]{0:T(128)} %media_slot.1, s32[32]{0:T(128)} %media_position.1, f32[1]{0:T(128)S(6)} %copy.15.gate_alpha, bf16[128,4096]{1,0:T(8,128)(2,1)} %queries.1, ...), custom_call_target="tpu_custom_call" | custom-call | tf_op jit(solution)/shard_map/backward/pallas_call | solution.py:746
  121.7 2.3 %hand_on.1 = (bf16[128,4096]{1,0:T(8,128)(2,1)}, bf16[4,1280]{1,0:T(4,128)(2,1)}, f32[40,256]{1,0:T(8,128)}, f32[40,256]{1,0:T(8,128)}) custom-call(bf16[128,4096]{1,0:T(8,128)(2,1)} %get-tuple-element.12.refs_0_, bf16[4,1280]{1,0:T(4,128)(2,1)} %get-tuple-element.13.refs_1_, f32[40,256]{1,0:T(8,128)} %get-tuple-element.14.refs_2_, ...), custom_call_target="tpu_custom_call" | custom-call | tf_op jit(solution)/shard_map/hand_on/pallas_call | solution.py:759
